TPU v7x, 32 devices: a whole 2x2x4 slice. The times are simulated.
32 devices in a mesh: row: 8 (over z, x), col: 4 (over y, core).
Axes of the slice: x: 2, y: 2, z: 4, core: 2. Of those that a mesh axis runs over, the one named last changes fastest.
Arguments:
- vectors: bfloat16 [256, 16384], P('col', 'row'), may hold values from -6 to 6
- hblocks: bfloat16 [256, 12, 4096], P('row'), may hold values from -0.15625 to 0.15625
- counts: int32 [256], P('row'), may hold values from 3 to 12, as said below
- sources: int32 [256, 12], P('row'), may hold values from 0 to 47, as said below
- send_rows: int32 [128], P('row'), may hold values from 0 to 31
Outputs:
- filtered: bfloat16 [256, 16384], P('col', 'row')
- gram_matrix: float32 [256, 256], P(None, 'col')
- projected: float32 [256, 256], P(None, 'col')
Inputs may be any that keep to these rules, and one draw needn't show every extreme that they name: Blocks 0 to counts[i] - 1 of block row i are live; the rows of every device include one with 12 live blocks. `sources`: entry 0 of block row i is i's own index within its device. On every device each slot value 32 + s, s below 16, stands exactly once, at block 1 or 2 of some row. `send_rows`: entries p * 16 + q * 2 + c name block rows of device p within it.
All inputs are finite; a program needn't handle non-finite values.
Results may differ from a plain program's by a relative error of at most 0.017.
Values may be sent and summed in bfloat16 or wider, within the bound.
A program may use at most 128 MiB of HBM per device.

v0:
```python
import functools

import jax
import jax.numpy as jnp
from jax import lax
from jax.experimental import pallas as pl
from jax.experimental.pallas import tpu as pltpu
from jax.sharding import PartitionSpec as P

B = 64
K = 12
PAIR = 2 * B
TILE = 256

center_value = 0.25
half_width = 1.5

MESH = pl.DeviceIdType.MESH
NN = (((1,), (0,)), ((), ()))
NT = (((1,), (1,)), ((), ()))


def dot(a, b, dims):
    return lax.dot_general(a, b, dims, preferred_element_type=jnp.float32)


def filter_kernel(
    n_row, n_col, send_rows, mask, x0, u,
    filtered, gram, projected,
    step_one, stacked, total, blocks, spread, out_buf, in_buf, gathered,
    piece_out, piece_in, sum_out, sum_in,
    send_sem, recv_sem, col_send, col_recv, piece_send, piece_recv, sum_send, sum_recv,
):
    me = lax.axis_index("row")
    mine = lax.axis_index("col")
    cols, length = x0.shape
    pairs = length // PAIR
    slots = 2 * n_row

    barrier = pltpu.get_barrier_semaphore()
    for step in range(1, n_row):
        pl.semaphore_signal(barrier, inc=1, device_id={"row": lax.rem(me + step, n_row)}, device_id_type=MESH)
    for step in range(1, n_col):
        pl.semaphore_signal(barrier, inc=1, device_id={"col": lax.rem(mine + step, n_col)}, device_id_type=MESH)
    pl.semaphore_wait(barrier, n_row + n_col - 2)

    lane = lax.broadcasted_iota(jnp.int32, (cols, PAIR), 1)
    low = lane < B

    def columns(index, width):
        return pl.ds(pl.multiple_of(index * width, width), width)

    def both(values):
        turned = pltpu.roll(values, B, 1)
        return jnp.where(low, values, turned), jnp.where(low, turned, values)

    def keep_blocks(pair, values):
        first, second = both(values)
        blocks[2 * pair] = first.astype(jnp.bfloat16)
        blocks[2 * pair + 1] = second.astype(jnp.bfloat16)

    def start_body(pair, carry):
        keep_blocks(pair, x0[:, columns(pair, PAIR)].astype(jnp.float32))
        return carry

    lax.fori_loop(0, pairs, start_body, 0)

    def row_copy(phase, slot_here, slot_there, peer):
        return pltpu.make_async_remote_copy(
            src_ref=out_buf.at[phase, slot_here],
            dst_ref=in_buf.at[phase, slot_there],
            send_sem=send_sem.at[phase, slot_here],
            recv_sem=recv_sem.at[phase, slot_there],
            device_id={"row": peer},
            device_id_type=MESH,
        )

    def apply_operator(phase, source, finish):
        def gather_body(peer, carry):
            first = blocks[send_rows[2 * peer]].astype(jnp.float32)
            second = blocks[send_rows[2 * peer + 1]].astype(jnp.float32)
            out_buf[phase, peer, :, pl.ds(0, PAIR)] = jnp.where(low, first, second).astype(jnp.bfloat16)
            return carry

        lax.fori_loop(0, n_row, gather_body, 0)

        def mirror_body(tile, carry):
            here = pl.ds(pl.multiple_of(length + tile * TILE, TILE), TILE)
            product = dot(source[...], u[:, here], NN).astype(jnp.bfloat16)
            out_buf[phase, 2 * tile, :, pl.ds(PAIR, PAIR)] = product[:, :PAIR]
            out_buf[phase, 2 * tile + 1, :, pl.ds(PAIR, PAIR)] = product[:, PAIR:]
            return carry

        lax.fori_loop(0, n_row // 2, mirror_body, 0)
        for step in range(1, n_row):
            peer = lax.rem(me + step, n_row)
            row_copy(phase, peer, me, peer).start()
        in_buf[phase, me] = out_buf[phase, me]

        def local_body(tile, carry):
            here = columns(tile, TILE)
            total[:, here] = dot(source[...], u[:, here], NN) + dot(source[...], u[here, pl.ds(0, length)], NT)
            return carry

        lax.fori_loop(0, length // TILE, local_body, 0)
        for step in range(1, n_row):
            peer = lax.rem(me + step, n_row)
            row_copy(phase, peer, peer, peer).wait_recv()

        arrived = jnp.concatenate([in_buf[phase, peer, :, pl.ds(0, PAIR)] for peer in range(n_row)], 1)

        def remote_body(tile, carry):
            here = columns(tile, TILE)
            total[:, here] += dot(arrived, u[here, pl.ds(length, slots * B)], NT)
            return carry

        lax.fori_loop(0, length // TILE, remote_body, 0)

        def spread_body(peer, carry):
            first, second = both(in_buf[phase, peer, :, pl.ds(PAIR, PAIR)].astype(jnp.float32))
            spread[2 * peer] = first
            spread[2 * peer + 1] = second
            return carry

        lax.fori_loop(0, n_row, spread_body, 0)

        def finish_body(pair, carry):
            here = columns(pair, PAIR)
            value = total[:, here]
            for slot in range(slots):
                value = value + spread[slot] * mask[pl.ds(slot, 1), here]
            finish(pair, here, value)
            return carry

        lax.fori_loop(0, pairs, finish_body, 0)
        for step in range(1, n_row):
            peer = lax.rem(me + step, n_row)
            row_copy(phase, peer, me, peer).wait_send()

    def first_finish(pair, here, value):
        new = ((value - center_value * x0[:, here].astype(jnp.float32)) / half_width).astype(jnp.bfloat16)
        step_one[:, here] = new
        keep_blocks(pair, new.astype(jnp.float32))

    def second_finish(pair, here, value):
        old = step_one[:, here].astype(jnp.float32)
        new = (
            2.0 * (value - center_value * old) / half_width - x0[:, here].astype(jnp.float32)
        ).astype(jnp.bfloat16)
        stacked[pl.ds(0, cols), here] = new
        gathered[mine, :, here] = new
        filtered[:, here] = new
        keep_blocks(pair, new.astype(jnp.float32))

    def third_finish(pair, here, value):
        stacked[pl.ds(cols, cols), here] = value.astype(jnp.bfloat16)

    def col_copy(slot, peer):
        return pltpu.make_async_remote_copy(
            src_ref=gathered.at[mine],
            dst_ref=gathered.at[slot],
            send_sem=col_send.at[peer],
            recv_sem=col_recv.at[slot],
            device_id={"col": peer},
            device_id_type=MESH,
        )

    apply_operator(0, x0, first_finish)
    apply_operator(1, step_one, second_finish)
    for step in range(1, n_col):
        peer = lax.rem(mine + step, n_col)
        col_copy(mine, peer).start()
    apply_operator(2, stacked.at[pl.ds(0, cols)], third_finish)
    for step in range(1, n_col):
        peer = lax.rem(mine + step, n_col)
        col_copy(peer, peer).wait_recv()

    piece = n_col * cols // n_row

    for group in range(n_col):
        part = dot(gathered[group], stacked[...], NT)
        for inner in range(cols // piece):
            piece_out[group * (cols // piece) + inner] = part[inner * piece : (inner + 1) * piece].astype(piece_out.dtype)

    def piece_copy(slot_here, slot_there, peer):
        return pltpu.make_async_remote_copy(
            src_ref=piece_out.at[slot_here],
            dst_ref=piece_in.at[slot_there],
            send_sem=piece_send.at[slot_here],
            recv_sem=piece_recv.at[slot_there],
            device_id={"row": peer},
            device_id_type=MESH,
        )

    def sum_copy(slot_there, peer):
        return pltpu.make_async_remote_copy(
            src_ref=sum_out,
            dst_ref=sum_in.at[slot_there],
            send_sem=sum_send.at[peer],
            recv_sem=sum_recv.at[slot_there],
            device_id={"row": peer},
            device_id_type=MESH,
        )

    peers = [lax.rem(me + step, n_row) for step in range(1, n_row)]
    for peer in peers:
        piece_copy(peer, me, peer).start()
    piece_in[me] = piece_out[me]
    for peer in peers:
        piece_copy(peer, peer, peer).wait_recv()
    summed = piece_in[0].astype(jnp.float32)
    for peer in range(1, n_row):
        summed = summed + piece_in[peer].astype(jnp.float32)
    sum_out[...] = summed.astype(sum_out.dtype)
    for peer in peers:
        sum_copy(me, peer).start()
    sum_in[me] = sum_out[...]
    for peer in peers:
        sum_copy(peer, peer).wait_recv()
    for index in range(n_row):
        value = sum_in[index].astype(jnp.float32)
        gram[pl.ds(index * piece, piece), :] = value[:, :cols]
        projected[pl.ds(index * piece, piece), :] = value[:, cols:]

    for peer in peers:
        piece_copy(peer, me, peer).wait_send()
        sum_copy(me, peer).wait_send()
    for step in range(1, n_col):
        peer = lax.rem(mine + step, n_col)
        col_copy(mine, peer).wait_send()


def on_device(vectors, hblocks, counts, sources, send_rows):
    rows_here = hblocks.shape[0]
    cols, length = vectors.shape
    slots = send_rows.shape[0]
    n_row = lax.axis_size("row")
    n_col = lax.axis_size("col")
    assert slots == 2 * n_row
    live = lax.broadcasted_iota(jnp.int32, (rows_here, K), 1) < counts[:, None]
    hot = jax.nn.one_hot(jnp.where(live, sources, -1), rows_here + slots, dtype=jnp.bfloat16)
    u = jnp.einsum(
        "ikj,ikab->iajb", hot, hblocks.reshape(rows_here, K, B, B), preferred_element_type=jnp.float32
    ).astype(jnp.bfloat16).reshape(length, (rows_here + slots) * B)
    mask = jnp.repeat(jax.nn.one_hot(send_rows, rows_here, dtype=jnp.float32), B, axis=1)
    return run_filter(n_row, n_col, vectors, u, mask, send_rows)


def run_filter(n_row, n_col, vectors, u, mask, send_rows):
    cols, length = vectors.shape
    slots = send_rows.shape[0]
    total_cols = n_col * cols
    piece = total_cols // n_row
    sum_type = jnp.bfloat16 if piece % 16 == 0 else jnp.float32
    vmem = pl.BlockSpec(memory_space=pltpu.VMEM)
    dma = pltpu.SemaphoreType.DMA
    return pl.pallas_call(
        functools.partial(filter_kernel, n_row, n_col),
        out_shape=(
            jax.ShapeDtypeStruct((cols, length), jnp.bfloat16),
            jax.ShapeDtypeStruct((total_cols, cols), jnp.float32),
            jax.ShapeDtypeStruct((total_cols, cols), jnp.float32),
        ),
        in_specs=[pl.BlockSpec(memory_space=pltpu.SMEM), vmem, vmem, vmem],
        out_specs=(vmem, vmem, vmem),
        scratch_shapes=[
            pltpu.VMEM((cols, length), jnp.bfloat16),
            pltpu.VMEM((2 * cols, length), jnp.bfloat16),
            pltpu.VMEM((cols, length), jnp.float32),
            pltpu.VMEM((length // B, cols, PAIR), jnp.bfloat16),
            pltpu.VMEM((slots, cols, PAIR), jnp.float32),
            pltpu.VMEM((3, n_row, cols, 2 * PAIR), jnp.bfloat16),
            pltpu.VMEM((3, n_row, cols, 2 * PAIR), jnp.bfloat16),
            pltpu.VMEM((n_col, cols, length), jnp.bfloat16),
            pltpu.VMEM((n_row, piece, 2 * cols), sum_type),
            pltpu.VMEM((n_row, piece, 2 * cols), sum_type),
            pltpu.VMEM((piece, 2 * cols), sum_type),
            pltpu.VMEM((n_row, piece, 2 * cols), sum_type),
            dma((3, n_row)), dma((3, n_row)),
            dma((n_col,)), dma((n_col,)),
            dma((n_row,)), dma((n_row,)),
            dma((n_row,)), dma((n_row,)),
        ],
        compiler_params=pltpu.CompilerParams(
            collective_id=0, has_side_effects=True, vmem_limit_bytes=56 * 1024 * 1024
        ),
    )(send_rows, mask, vectors, u)


def solution(mesh):
    return jax.shard_map(
        on_device,
        mesh=mesh,
        in_specs=(P("col", "row"), P("row", None, None), P("row"), P("row", None), P("row")),
        out_specs=(P("col", "row"), P(None, "col"), P(None, "col")),
        check_vma=False,
    )
```

profile of v0, /device:TPU:0, one launch (start us, length us, event | category | flops | bytes accessed | tf_op | source)
XLA Modules:
  0.0 121.4 jit_solution(15372211433418521574)
XLA Ops:
  0.6 0.0 copy-start.2
  0.6 0.0 copy-start
  0.7 9.7 %reshape.19 = bf16[32,12,64,64]{3,2,0,1:T(8,128)(2,1)} reshape(bf16[32,12,4096]{2,0,1:T(8,128)(2,1)} %param.6) | data formatting | bytes 6291456 | tf_op jit(solution)/shard_map/reshape | solution.py:243
  10.3 0.0 copy-done.2
  10.3 0.0 copy-done
  10.3 0.1 copy.8
  10.4 13.8 %convert_bitcast_fusion = bf16[32,64,48,64]{3,2,1,0:T(8,128)(2,1)} fusion(bf16[32,12,64,64]{3,2,0,1:T(8,128)(2,1)} %reshape.19, s32[32,12]{1,0:T(8,128)S(1)} %copy.8), kind=kOutput, calls=%fused_computation | convolution fusion | flops 157304832 | bytes 15730176 | tf_op jit(solution)/shard_map/ikj,ikab->iajb/dot_general | solution.py:242
  24.2 0.0 copy-start.1
  24.2 31.5 %reshape.20.u = bf16[2048,3072]{1,0:T(8,128)(2,1)} reshape(bf16[32,64,48,64]{3,2,1,0:T(8,128)(2,1)} %convert_bitcast_fusion) | data formatting | bytes 25165824 | tf_op jit(solution)/shard_map/reshape | solution.py:244
  55.7 0.0 copy-done.1
  55.7 0.1 fusion.4
  55.7 0.1 broadcast_in_dim.12
  55.9 0.8 reshape.18.mask
  56.7 59.9 %shard_map.76 = (bf16[64,2048]{1,0:T(8,128)(2,1)}, f32[256,64]{1,0:T(8,128)}, f32[256,64]{1,0:T(8,128)}) custom-call(s32[16]{0:T(128)} %send_rows.1, f32[16,2048]{1,0:T(8,128)} %reshape.18.mask, bf16[64,2048]{1,0:T(8,128)(2,1)} %x0.1, bf16[2048,3072]{1,0:T(8,128)(2,1)} %reshape.20.u), custom_call_target="tpu_custom_call" | custom-call | tf_op jit(solution)/shard_map/pallas_call | solution.py:257
  116.5 1.6 %copy.10 = f32[256,64]{0,1:T(8,128)} copy(f32[256,64]{1,0:T(8,128)} %get-tuple-element.4) | data formatting | bytes 131072 | tf_op jit(solution)/shard_map/pallas_call | solution.py:257
  118.1 1.6 %copy.11 = f32[256,64]{0,1:T(8,128)} copy(f32[256,64]{1,0:T(8,128)} %get-tuple-element.5) | data formatting | bytes 131072 | tf_op jit(solution)/shard_map/pallas_call | solution.py:257
  119.8 1.7 %copy.16 = bf16[64,2048]{1,0:T(8,128)(2,1)} copy(bf16[64,2048]{1,0:T(8,128)(2,1)} %get-tuple-element.9) | data formatting | bytes 524288
  (1 shorter events, 0.0 us)
Async XLA Ops:
  0.6 9.7 %copy-start.2 = (s32[32]{0:T(128)S(1)}, s32[32]{0:T(128)}, u32[]{:S(2)}) copy-start(s32[32]{0:T(128)} %param.7) | copy-start | bytes 388
  0.6 9.7 %copy-start = (s32[32,12]{0,1:T(8,128)S(1)}, s32[32,12]{0,1:T(8,128)}, u32[]{:S(2)}) copy-start(s32[32,12]{0,1:T(8,128)} %param.8) | copy-start | bytes 4612
  24.2 31.5 %copy-start.1 = (s32[16]{0:T(128)S(1)}, s32[16]{0:T(128)}, u32[]{:S(2)}) copy-start(s32[16]{0:T(128)} %send_rows.1) | copy-start | bytes 196
where the time goes:
time: 123 us; the launch traced here: 121 us
  Pallas kernels  59.9 us (49%)
  local copies, waits for them, and re-layouts  47.1 us (38%)
  matrix products  13.8 us (11%)
    pallas_call x1, Pallas kernels, run_filter(): pl.pallas_call(functools.partial(filter_kernel, n_row, n_col), out_shape=...  59.9 us
    reshape x1, local copies, waits for them, and re-layouts, on_device(): u = jnp.einsum('ikj,ikab->iajb', hot, hblocks.reshape(rows_here, K, B, B)...  31.5 us
    dot_general x1, matrix products, on_device(): jnp.einsum('ikj,ikab->iajb', hot, hblocks.reshape(rows_here, K, B, B), pr...  13.8 us
    reshape x1, local copies, waits for them, and re-layouts, on_device(): hblocks.reshape(rows_here, K, B, B)  9.65 us
    pallas_call x2, local copies, waits for them, and re-layouts, run_filter(): pl.pallas_call(functools.partial(filter_kernel, n_row, n_col), out_shape=...  3.23 us

commit v1 on v0

v1 whole, which is shorter than its diff:
```python
import functools

import jax
import jax.numpy as jnp
from jax import lax
from jax.experimental import pallas as pl
from jax.experimental.pallas import tpu as pltpu
from jax.sharding import PartitionSpec as P

B = 64
K = 12
PAIR = 2 * B
TILE = 256
GROUP = 16
HALF = B // 2

center_value = 0.25
half_width = 1.5

MESH = pl.DeviceIdType.MESH
NN = (((1,), (0,)), ((), ()))
NT = (((1,), (1,)), ((), ()))


def dot(a, b, dims):
    return lax.dot_general(a, b, dims, preferred_element_type=jnp.float32)


def filter_kernel(
    n_row, n_col, chunk, index, key, x_in, h,
    filtered, gram, projected,
    ident, order, h_ordered, placed, upper, dense, diagonal, mask,
    x0, step_one, stacked, total, blocks, spread, upspread, out_buf, in_buf, gathered,
    piece_out, piece_in, sum_out, sum_in,
    send_sem, recv_sem, col_send, col_recv, piece_send, piece_recv, sum_send, sum_recv,
):
    me = lax.axis_index("row")
    mine = lax.axis_index("col")
    cols, length = x_in.shape
    rows = length // B
    pairs = length // PAIR
    slots = 2 * n_row
    named = rows + slots
    halves = named // 2
    tiles = length // TILE
    bf16 = jnp.bfloat16
    f32 = jnp.float32

    barrier = pltpu.get_barrier_semaphore()
    for step in range(1, n_row):
        pl.semaphore_signal(barrier, inc=1, device_id={"row": lax.rem(me + step, n_row)}, device_id_type=MESH)
    for step in range(1, n_col):
        pl.semaphore_signal(barrier, inc=1, device_id={"col": lax.rem(mine + step, n_col)}, device_id_type=MESH)

    def columns(at, width):
        return pl.ds(pl.multiple_of(at * width, width), width)

    def low_half(count):
        return lax.broadcasted_iota(jnp.int32, (count, PAIR), 1) < B

    low = low_half(cols)

    def both(values, where_low=low):
        turned = pltpu.roll(values, B, 1)
        return jnp.where(where_low, values, turned), jnp.where(where_low, turned, values)

    row_at = lax.broadcasted_iota(jnp.int32, (TILE, TILE), 0)
    col_at = lax.broadcasted_iota(jnp.int32, (TILE, TILE), 1)
    within = row_at & (B - 1)
    target = (row_at - within) + (within & 1) * HALF + (within >> 1)
    order[...] = jnp.where(target == col_at, 1.0, 0.0).astype(bf16)
    ident[...] = jnp.where(row_at == col_at, 1.0, 0.0).astype(bf16)

    lane_block = lax.broadcasted_iota(jnp.int32, (1, length), 1) >> 6

    def mask_body(slot, carry):
        mask[pl.ds(slot, 1), :] = jnp.where(lane_block == index[slot], 1.0, 0.0)
        return carry

    lax.fori_loop(0, slots, mask_body, 0)

    def keep_blocks(pair, values):
        first, second = both(values)
        blocks[2 * pair] = first.astype(bf16)
        blocks[2 * pair + 1] = second.astype(bf16)

    for tile in range(tiles):
        here = pl.ds(tile * TILE, TILE)
        value = dot(x_in[:, here], order[...], NN)
        x0[:, here] = value.astype(bf16)
        keep_blocks(2 * tile, value[:, :PAIR])
        keep_blocks(2 * tile + 1, value[:, PAIR:])

    def order_body(tile, carry):
        here = columns(tile, TILE)
        for group in range(rows // GROUP):
            part = h[:, pl.ds(group * GROUP, GROUP), here].reshape(K * GROUP, TILE)
            h_ordered[group, :, here] = dot(part, order[...], NN).astype(bf16)
        return carry

    lax.fori_loop(0, B * B // TILE, order_body, 0)

    count = chunk * named
    stride = count + 8
    per_group = GROUP // chunk
    low_rows = low_half(HALF)

    def chunk_body(at, carry):
        group = at // per_group
        inner = at % per_group
        names = lax.broadcasted_iota(jnp.int32, (count, K * GROUP), 0) + inner * count
        hot = jnp.where(names == key[group], 1.0, 0.0).astype(bf16)

        def place_body(tile, carry):
            value = dot(hot, h_ordered[group, :, columns(tile, TILE)], NN)
            placed[pl.ds(pl.multiple_of(2 * tile * stride, 8), count), :] = value[:, :PAIR]
            placed[pl.ds(pl.multiple_of((2 * tile + 1) * stride, 8), count), :] = value[:, PAIR:]
            return carry

        lax.fori_loop(0, B * B // TILE, place_body, 0)

        def turn_body(row, carry):
            for pair in range(halves):
                base = row * named + pair
                first = placed[pl.ds(base, HALF, stride=stride), :]
                second = placed[pl.ds(base + halves, HALF, stride=stride), :]
                even = jnp.where(low_rows, first, pltpu.roll(second, B, 1))
                odd = jnp.where(low_rows, pltpu.roll(first, B, 1), second)
                here = pl.ds(pair * PAIR, PAIR)
                upper[at * chunk + row, pl.ds(0, HALF), here] = even.astype(bf16)
                upper[at * chunk + row, pl.ds(HALF, HALF), here] = odd.astype(bf16)
            return carry

        lax.fori_loop(0, chunk, turn_body, 0)
        return carry

    lax.fori_loop(0, rows // chunk, chunk_body, 0)

    low_block = low_half(B)
    diagonal[...] = jnp.zeros_like(diagonal)
    for slot in range(slots):
        here = pl.ds(length + (slot // 2) * PAIR, PAIR)
        value = upper[index[slots + slot], :, here].astype(f32)
        keep = low_block if slot % 2 == 0 else jnp.logical_not(low_block)
        part = slot % 4
        diagonal[slot // 4, pl.ds(part * B, B), pl.ds((part // 2) * PAIR, PAIR)] = jnp.where(keep, value, 0.0).astype(bf16)

    per_tile = TILE // B

    def dense_body(tile, carry):
        for other in range(tiles):
            there = upper[pl.ds(other * per_tile, per_tile), :, columns(tile, TILE)].reshape(TILE, TILE)
            straight = upper[pl.ds(tile * per_tile, per_tile), :, pl.ds(other * TILE, TILE)].reshape(TILE, TILE)
            value = dot(ident[...], there, NT) + straight.astype(f32)
            dense[columns(tile, TILE), pl.ds(other * TILE, TILE)] = value.astype(bf16)
        return carry

    lax.fori_loop(0, tiles, dense_body, 0)
    upspread[slots] = jnp.zeros((cols, PAIR), f32)

    pl.semaphore_wait(barrier, n_row + n_col - 2)

    def row_copy(phase, slot_here, slot_there, peer):
        return pltpu.make_async_remote_copy(
            src_ref=out_buf.at[phase, slot_here],
            dst_ref=in_buf.at[phase, slot_there],
            send_sem=send_sem.at[phase, slot_here],
            recv_sem=recv_sem.at[phase, slot_there],
            device_id={"row": peer},
            device_id_type=MESH,
        )

    def pick(first, second):
        return jnp.where(low, blocks[first].astype(f32), blocks[second].astype(f32)).astype(bf16)

    def apply_operator(phase, source, finish, beside):
        for pack in range(slots // 4):
            at = slots + 4 * pack
            near = jnp.concatenate([pick(index[at], index[at + 1]), pick(index[at + 2], index[at + 3])], 1)
            product = dot(near, diagonal[pack], NN).astype(bf16)
            for inner in range(2):
                peer = 2 * pack + inner
                out_buf[phase, peer, :, pl.ds(0, PAIR)] = pick(index[2 * peer], index[2 * peer + 1])
                out_buf[phase, peer, :, pl.ds(PAIR, PAIR)] = product[:, inner * PAIR : (inner + 1) * PAIR]
        for step in range(1, n_row):
            peer = lax.rem(me + step, n_row)
            row_copy(phase, peer, me, peer).start()
        in_buf[phase, me] = out_buf[phase, me]

        def local_body(tile, carry):
            here = columns(tile, TILE)
            total[:, here] = dot(source[...], dense[:, here], NN)
            return carry

        lax.fori_loop(0, tiles, local_body, 0)
        beside()
        for step in range(1, n_row):
            peer = lax.rem(me + step, n_row)
            row_copy(phase, peer, peer, peer).wait_recv()

        for pack in range(slots // 4):
            far = jnp.concatenate([in_buf[phase, 2 * pack + inner, :, pl.ds(0, PAIR)] for inner in range(2)], 1)
            product = dot(far, diagonal[pack], NT)
            for inner in range(2):
                peer = 2 * pack + inner
                first, second = both(product[:, inner * PAIR : (inner + 1) * PAIR])
                upspread[2 * peer] = first
                upspread[2 * peer + 1] = second
                first, second = both(in_buf[phase, peer, :, pl.ds(PAIR, PAIR)].astype(f32))
                spread[2 * peer] = first
                spread[2 * peer + 1] = second

        def finish_body(pair, carry):
            here = columns(pair, PAIR)
            at = 2 * slots + 4 * pair
            value = total[:, here] + jnp.where(
                low,
                upspread[index[at]] + upspread[index[at + 1]],
                upspread[index[at + 2]] + upspread[index[at + 3]],
            )
            for slot in range(slots):
                value = value + spread[slot] * mask[pl.ds(slot, 1), here]
            finish(pair, here, value)
            return carry

        lax.fori_loop(0, pairs, finish_body, 0)

    def first_finish(pair, here, value):
        new = ((value - center_value * x0[:, here].astype(f32)) / half_width).astype(bf16)
        step_one[:, here] = new
        keep_blocks(pair, new.astype(f32))

    def second_finish(pair, here, value):
        old = step_one[:, here].astype(f32)
        new = (2.0 * (value - center_value * old) / half_width - x0[:, here].astype(f32)).astype(bf16)
        stacked[pl.ds(0, cols), here] = new
        gathered[mine, :, here] = new
        keep_blocks(pair, new.astype(f32))

    def third_finish(pair, here, value):
        stacked[pl.ds(cols, cols), here] = value.astype(bf16)

    def nothing():
        pass

    def write_filtered():
        for tile in range(tiles):
            here = pl.ds(tile * TILE, TILE)
            filtered[:, here] = dot(stacked[pl.ds(0, cols), here], order[...], NT).astype(bf16)

    def col_copy(slot, peer):
        return pltpu.make_async_remote_copy(
            src_ref=gathered.at[mine],
            dst_ref=gathered.at[slot],
            send_sem=col_send.at[peer],
            recv_sem=col_recv.at[slot],
            device_id={"col": peer},
            device_id_type=MESH,
        )

    apply_operator(0, x0, first_finish, nothing)
    apply_operator(1, step_one, second_finish, nothing)
    for step in range(1, n_col):
        peer = lax.rem(mine + step, n_col)
        col_copy(mine, peer).start()
    apply_operator(2, stacked.at[pl.ds(0, cols)], third_finish, write_filtered)
    for step in range(1, n_col):
        peer = lax.rem(mine + step, n_col)
        col_copy(peer, peer).wait_recv()

    piece = 2 * cols // n_row
    part = dot(stacked[...], gathered[...].reshape(n_col * cols, length), NT)
    for at in range(n_row):
        piece_out[at] = part[at * piece : (at + 1) * piece].astype(piece_out.dtype)

    def piece_copy(slot_here, slot_there, peer):
        return pltpu.make_async_remote_copy(
            src_ref=piece_out.at[slot_here],
            dst_ref=piece_in.at[slot_there],
            send_sem=piece_send.at[slot_here],
            recv_sem=piece_recv.at[slot_there],
            device_id={"row": peer},
            device_id_type=MESH,
        )

    def sum_copy(slot_there, peer):
        return pltpu.make_async_remote_copy(
            src_ref=sum_out,
            dst_ref=sum_in.at[slot_there],
            send_sem=sum_send.at[peer],
            recv_sem=sum_recv.at[slot_there],
            device_id={"row": peer},
            device_id_type=MESH,
        )

    peers = [lax.rem(me + step, n_row) for step in range(1, n_row)]
    for peer in peers:
        piece_copy(peer, me, peer).start()
    piece_in[me] = piece_out[me]
    for peer in peers:
        piece_copy(peer, peer, peer).wait_recv()
    summed = piece_in[0].astype(f32)
    for peer in range(1, n_row):
        summed = summed + piece_in[peer].astype(f32)
    sum_out[...] = summed.astype(sum_out.dtype)
    for peer in peers:
        sum_copy(me, peer).start()
    sum_in[me] = sum_out[...]
    for peer in peers:
        sum_copy(peer, peer).wait_recv()
    for at in range(n_row):
        value = sum_in[at].astype(f32)
        first = at * piece
        if first < cols:
            gram[pl.ds(first, piece), :] = value
        else:
            projected[pl.ds(first - cols, piece), :] = value

    for peer in peers:
        for phase in range(3):
            row_copy(phase, peer, me, peer).wait_send()
        piece_copy(peer, me, peer).wait_send()
        sum_copy(me, peer).wait_send()
    for step in range(1, n_col):
        peer = lax.rem(mine + step, n_col)
        col_copy(mine, peer).wait_send()


def on_device(vectors, hblocks, counts, sources, send_rows):
    rows = hblocks.shape[0]
    cols, length = vectors.shape
    slots = send_rows.shape[0]
    n_row = lax.axis_size("row")
    n_col = lax.axis_size("col")
    assert slots == 2 * n_row
    named = rows + slots
    live = lax.broadcasted_iota(jnp.int32, (rows, K), 1) < counts[:, None]
    place = (jnp.arange(rows, dtype=jnp.int32) % GROUP)[:, None] * named
    key = jnp.where(live, place + (sources % 2) * (named // 2) + sources // 2, -1)
    key = key.reshape(rows // GROUP, GROUP, K).transpose(0, 2, 1).reshape(rows // GROUP, 1, K * GROUP)
    near = sources[:, 1:3]
    which = near[:, :, None] == rows + jnp.arange(slots, dtype=jnp.int32)
    holder = jnp.sum(jnp.where(which, jnp.arange(rows, dtype=jnp.int32)[:, None, None], 0), (0, 1), dtype=jnp.int32)
    entry = jnp.where(near >= rows, near - rows, slots).reshape(-1)
    index = jnp.concatenate([send_rows, holder, entry])

    total_cols = n_col * cols
    piece = 2 * cols // n_row
    sum_type = jnp.bfloat16 if piece % 16 == 0 else jnp.float32
    chunk = 8 if named <= 48 else 4
    vmem = pl.BlockSpec(memory_space=pltpu.VMEM)
    dma = pltpu.SemaphoreType.DMA
    bf16 = jnp.bfloat16
    f32 = jnp.float32
    filtered, gram, projected = pl.pallas_call(
        functools.partial(filter_kernel, n_row, n_col, chunk),
        out_shape=(
            jax.ShapeDtypeStruct((cols, length), bf16),
            jax.ShapeDtypeStruct((cols, total_cols), f32),
            jax.ShapeDtypeStruct((cols, total_cols), f32),
        ),
        in_specs=[pl.BlockSpec(memory_space=pltpu.SMEM), vmem, vmem, vmem],
        out_specs=(vmem, vmem, vmem),
        scratch_shapes=[
            pltpu.VMEM((TILE, TILE), bf16),
            pltpu.VMEM((TILE, TILE), bf16),
            pltpu.VMEM((rows // GROUP, K * GROUP, B * B), bf16),
            pltpu.VMEM((HALF * (chunk * named + 8), PAIR), f32),
            pltpu.VMEM((rows, B, named * B), bf16),
            pltpu.VMEM((length, length), bf16),
            pltpu.VMEM((slots // 4, TILE, TILE), bf16),
            pltpu.VMEM((slots, length), f32),
            pltpu.VMEM((cols, length), bf16),
            pltpu.VMEM((cols, length), bf16),
            pltpu.VMEM((2 * cols, length), bf16),
            pltpu.VMEM((cols, length), f32),
            pltpu.VMEM((rows, cols, PAIR), bf16),
            pltpu.VMEM((slots, cols, PAIR), f32),
            pltpu.VMEM((slots + 1, cols, PAIR), f32),
            pltpu.VMEM((3, n_row, cols, 2 * PAIR), bf16),
            pltpu.VMEM((3, n_row, cols, 2 * PAIR), bf16),
            pltpu.VMEM((n_col, cols, length), bf16),
            pltpu.VMEM((n_row, piece, total_cols), sum_type),
            pltpu.VMEM((n_row, piece, total_cols), sum_type),
            pltpu.VMEM((piece, total_cols), sum_type),
            pltpu.VMEM((n_row, piece, total_cols), sum_type),
            dma((3, n_row)), dma((3, n_row)),
            dma((n_col,)), dma((n_col,)),
            dma((n_row,)), dma((n_row,)),
            dma((n_row,)), dma((n_row,)),
        ],
        compiler_params=pltpu.CompilerParams(
            collective_id=0, has_side_effects=True, vmem_limit_bytes=60 * 1024 * 1024
        ),
    )(index, key, vectors, hblocks.transpose(1, 0, 2))
    return filtered, gram.T, projected.T


def solution(mesh):
    return jax.shard_map(
        on_device,
        mesh=mesh,
        in_specs=(P("col", "row"), P("row", None, None), P("row"), P("row", None), P("row")),
        out_specs=(P("col", "row"), P(None, "col"), P(None, "col")),
        check_vma=False,
    )
```

time: 123 us -> 83.1 us (0.68)
  the two profiles are of different devices: /device:TPU:0 before, /device:TPU:1 now
where the time goes in v1:
time: 83.1 us; the launch traced here: 82.7 us
  Pallas kernels  73.7 us (89%)
  local copies, waits for them, and re-layouts  5.55 us (7%)
  other arithmetic  2.85 us (3%)
    pallas_call x1, Pallas kernels, on_device(): pl.pallas_call(functools.partial(filter_kernel, n_row, n_col, chunk), out...  73.7 us
    unnamed x3, local copies, waits for them, and re-layouts  4.61 us

profile of v1, /device:TPU:1, one launch (start us, length us, event | category | flops | bytes accessed | tf_op | source)
XLA Modules:
  0.0 82.7 jit_solution(8974756417970394281)
XLA Ops:
  0.7 0.7 fusion.9
  1.3 0.2 select_reduce_fusion
  1.5 0.7 fusion.3
  2.2 0.1 reshape.33
  2.3 0.7 reshape.35.key
  3.0 0.1 copy.15
  3.1 0.1 reshape.32
  3.2 1.2 %pad_add_fusion.index = s32[96]{0:T(128)} fusion(s32[64]{0:T(128)S(1)} %reshape.32, s32[16]{0:T(128)S(1)} %select_reduce_fusion, s32[16]{0:T(128)} %param.9), kind=kLoop, calls=%fused_computation.20 | loop fusion | flops 192 | bytes 768 | tf_op jit(solution)/shard_map/concatenate | solution.py:345
  4.4 73.7 %shard_map.76 = (bf16[64,2048]{1,0:T(8,128)(2,1)}, f32[64,256]{1,0:T(8,128)}, f32[64,256]{1,0:T(8,128)}) custom-call(s32[96]{0:T(128)} %pad_add_fusion.index, s32[2,1,192]{2,1,0:T(1,128)} %reshape.35.key, bf16[64,2048]{1,0:T(8,128)(2,1)} %x_in.1, bf16[12,32,4096]{2,1,0:T(8,128)(2,1)} %bitcast.8), custom_call_target="tpu_custom_call" | custom-call | tf_op jit(solution)/shard_map/pallas_call | solution.py:355
  78.1 1.7 %copy.23 = bf16[64,2048]{1,0:T(8,128)(2,1)} copy(bf16[64,2048]{1,0:T(8,128)(2,1)} %get-tuple-element.14) | data formatting | bytes 524288
  79.8 1.5 %copy.24 = f32[256,64]{0,1:T(8,128)} copy(f32[256,64]{0,1:T(8,128)} %bitcast.11) | data formatting | bytes 131072
  81.3 1.5 %copy.25 = f32[256,64]{0,1:T(8,128)} copy(f32[256,64]{0,1:T(8,128)} %bitcast.10) | data formatting | bytes 131072
  (3 shorter events, 0.0 us)

commit v2 on v1

v2 whole, which is shorter than its diff:
```python
import functools

import jax
import jax.numpy as jnp
from jax import lax
from jax.experimental import pallas as pl
from jax.experimental.pallas import tpu as pltpu
from jax.sharding import PartitionSpec as P

B = 64
K = 12
PAIR = 2 * B
TILE = 256
UNROLL = 4
HALF = B // 2

center_value = 0.25
half_width = 1.5

MESH = pl.DeviceIdType.MESH
NN = (((1,), (0,)), ((), ()))
NT = (((1,), (1,)), ((), ()))


def dot(a, b, dims):
    return lax.dot_general(a, b, dims, preferred_element_type=jnp.float32)


def order_matrix():
    row_at = lax.broadcasted_iota(jnp.int32, (TILE, TILE), 0)
    col_at = lax.broadcasted_iota(jnp.int32, (TILE, TILE), 1)
    within = row_at & (B - 1)
    target = (row_at - within) + (within & 1) * HALF + (within >> 1)
    return jnp.where(target == col_at, 1.0, 0.0).astype(jnp.bfloat16)


def build_kernel(rows, slots, sources, counts, h, dense, diagonal, holder, order, ident, placed, upper):
    step = pl.program_id(0)
    per_tile = TILE // B
    tiles = rows // per_tile
    stride = rows + 8
    bf16 = jnp.bfloat16

    @pl.when(step == 0)
    def _():
        order[...] = order_matrix()
        row_at = lax.broadcasted_iota(jnp.int32, (TILE, TILE), 0)
        col_at = lax.broadcasted_iota(jnp.int32, (TILE, TILE), 1)
        ident[...] = jnp.where(row_at == col_at, 1.0, 0.0).astype(bf16)
        diagonal[...] = jnp.zeros_like(diagonal)

        def clear_body(row, carry):
            upper[row] = jnp.zeros_like(upper[row])
            return carry

        lax.fori_loop(0, rows, clear_body, 0)

        def holder_body(row, carry):
            for slot in (1, 2):
                source = sources[slot, row]

                @pl.when(source >= rows)
                def _():
                    holder[source - rows] = row

            return carry

        lax.fori_loop(0, rows, holder_body, 0)

    @pl.when(step < K)
    def _():
        pieces = B * B // TILE
        lanes = jnp.concatenate([h[0, :, at * TILE : (at + 1) * TILE] for at in range(pieces)], 0)
        value = dot(lanes, order[...], NN)
        for at in range(pieces):
            part = value[at * rows : (at + 1) * rows]
            placed[pl.ds(2 * at * stride, rows), :] = part[:, :PAIR]
            placed[pl.ds((2 * at + 1) * stride, rows), :] = part[:, PAIR:]
        side = lax.broadcasted_iota(jnp.int32, (HALF, PAIR), 1) >> 6

        def add_body(group, carry):
            news = []
            for inner in range(UNROLL):
                row = group * UNROLL + inner
                source = sources[step, row]
                half = source & 1
                wanted = jnp.where(step < counts[row], half, 2)
                straight = placed[pl.ds(row, HALF, stride=stride), :]
                turned = pltpu.roll(straight, B, 1)
                keep = side == wanted
                first = jnp.broadcast_to(half, (HALF, PAIR)) == 0
                even = jnp.where(keep, jnp.where(first, straight, turned), 0.0)
                odd = jnp.where(keep, jnp.where(first, turned, straight), 0.0)
                old = upper[row, source >> 1]
                news.append((row, source >> 1, old + jnp.concatenate([even, odd], 0).astype(bf16)))
            for row, pair, new in news:
                upper[row, pair] = new
            return carry

        lax.fori_loop(0, rows // UNROLL, add_body, 0)

    @pl.when(step >= K)
    def _():
        tile = step - K
        for other in range(tiles):
            def block(at_row, at_col):
                return jnp.concatenate(
                    [
                        upper[pl.ds(at_row * per_tile, per_tile), 2 * at_col + side].reshape(TILE, PAIR)
                        for side in range(2)
                    ],
                    1,
                )

            value = dot(ident[...], block(tile, other), NT) + block(other, tile).astype(jnp.float32)
            dense[0, pl.ds(other * TILE, TILE), :] = value.astype(bf16)

    @pl.when(step == K + tiles - 1)
    def _():
        low = lax.broadcasted_iota(jnp.int32, (B, PAIR), 1) < B
        for slot in range(slots):
            value = upper[holder[slot], (rows + slot) // 2].astype(jnp.float32)
            keep = low if slot % 2 == 0 else jnp.logical_not(low)
            part = slot % 4
            diagonal[slot // 4, pl.ds(part * B, B), pl.ds((part // 2) * PAIR, PAIR)] = jnp.where(
                keep, value, 0.0
            ).astype(bf16)


def output_kernel(cols, ordered, sums, filtered, gram, projected):
    order = order_matrix()
    for tile in range(ordered.shape[1] // TILE):
        here = pl.ds(tile * TILE, TILE)
        filtered[:, here] = dot(ordered[:, here], order, NT).astype(jnp.bfloat16)
    count, piece = sums.shape[0], sums.shape[1]
    for at in range(count):
        value = sums[at].astype(jnp.float32)
        first = at * piece
        if first < cols:
            gram[pl.ds(first, piece), :] = value
        else:
            projected[pl.ds(first - cols, piece), :] = value


def filter_kernel(
    n_row, n_col, send_rows, sources, holder, x_in, diagonal, dense_in,
    filtered, sum_in,
    dense, mask,
    x0, step_one, stacked, total, blocks, spread, upspread, out_buf, in_buf, gathered,
    piece_out, piece_in, sum_out,
    dense_sem,
    send_sem, recv_sem, col_send, col_recv, piece_send, piece_recv, sum_send, sum_recv,
):
    me = lax.axis_index("row")
    mine = lax.axis_index("col")
    cols, length = x_in.shape
    rows = length // B
    pairs = length // PAIR
    slots = 2 * n_row
    tiles = length // TILE
    bf16 = jnp.bfloat16
    f32 = jnp.float32

    barrier = pltpu.get_barrier_semaphore()
    for step in range(1, n_row):
        pl.semaphore_signal(barrier, inc=1, device_id={"row": lax.rem(me + step, n_row)}, device_id_type=MESH)
    for step in range(1, n_col):
        pl.semaphore_signal(barrier, inc=1, device_id={"col": lax.rem(mine + step, n_col)}, device_id_type=MESH)

    def dense_copy(tile):
        return pltpu.make_async_copy(dense_in.at[tile], dense.at[tile], dense_sem.at[tile])

    for tile in range(tiles):
        dense_copy(tile).start()

    def columns(at, width):
        return pl.ds(pl.multiple_of(at * width, width), width)

    low = lax.broadcasted_iota(jnp.int32, (cols, PAIR), 1) < B

    def both(values):
        turned = pltpu.roll(values, B, 1)
        return jnp.where(low, values, turned), jnp.where(low, turned, values)

    lane_block = lax.broadcasted_iota(jnp.int32, (1, length), 1) >> 6

    def mask_body(slot, carry):
        mask[pl.ds(slot, 1), :] = jnp.where(lane_block == send_rows[slot], 1.0, 0.0)
        return carry

    lax.fori_loop(0, slots, mask_body, 0)

    def keep_blocks(pair, values):
        first, second = both(values)
        blocks[2 * pair] = first.astype(bf16)
        blocks[2 * pair + 1] = second.astype(bf16)

    order = order_matrix()
    for tile in range(tiles):
        here = pl.ds(tile * TILE, TILE)
        value = dot(x_in[:, here], order, NN)
        x0[:, here] = value.astype(bf16)
        keep_blocks(2 * tile, value[:, :PAIR])
        keep_blocks(2 * tile + 1, value[:, PAIR:])

    upspread[slots] = jnp.zeros((cols, PAIR), f32)

    def arrived_at(row, slot):
        source = sources[slot, row]
        return upspread[jnp.where(source >= rows, source - rows, slots)]

    pl.semaphore_wait(barrier, n_row + n_col - 2)

    def row_copy(phase, slot_here, slot_there, peer):
        return pltpu.make_async_remote_copy(
            src_ref=out_buf.at[phase, slot_here],
            dst_ref=in_buf.at[phase, slot_there],
            send_sem=send_sem.at[phase, slot_here],
            recv_sem=recv_sem.at[phase, slot_there],
            device_id={"row": peer},
            device_id_type=MESH,
        )

    def pick(first, second):
        return jnp.where(low, blocks[first].astype(f32), blocks[second].astype(f32)).astype(bf16)

    def apply_operator(phase, source, finish):
        for pack in range(slots // 4):
            at = 4 * pack
            near = jnp.concatenate([pick(holder[at], holder[at + 1]), pick(holder[at + 2], holder[at + 3])], 1)
            product = dot(near, diagonal[pack], NN).astype(bf16)
            for inner in range(2):
                peer = 2 * pack + inner
                out_buf[phase, peer, :, pl.ds(0, PAIR)] = pick(send_rows[2 * peer], send_rows[2 * peer + 1])
                out_buf[phase, peer, :, pl.ds(PAIR, PAIR)] = product[:, inner * PAIR : (inner + 1) * PAIR]
        for step in range(1, n_row):
            peer = lax.rem(me + step, n_row)
            row_copy(phase, peer, me, peer).start()
        in_buf[phase, me] = out_buf[phase, me]

        def local_body(tile, carry):
            if phase == 0:
                dense_copy(tile).wait()
            total[:, columns(tile, TILE)] = dot(source[...], dense[tile], NN)
            return carry

        lax.fori_loop(0, tiles, local_body, 0)
        for step in range(1, n_row):
            peer = lax.rem(me + step, n_row)
            row_copy(phase, peer, peer, peer).wait_recv()

        for pack in range(slots // 4):
            far = jnp.concatenate([in_buf[phase, 2 * pack + inner, :, pl.ds(0, PAIR)] for inner in range(2)], 1)
            product = dot(far, diagonal[pack], NT)
            for inner in range(2):
                peer = 2 * pack + inner
                first, second = both(product[:, inner * PAIR : (inner + 1) * PAIR])
                upspread[2 * peer] = first
                upspread[2 * peer + 1] = second
                first, second = both(in_buf[phase, peer, :, pl.ds(PAIR, PAIR)].astype(f32))
                spread[2 * peer] = first
                spread[2 * peer + 1] = second

        def finish_body(pair, carry):
            here = columns(pair, PAIR)
            value = total[:, here] + jnp.where(
                low,
                arrived_at(2 * pair, 1) + arrived_at(2 * pair, 2),
                arrived_at(2 * pair + 1, 1) + arrived_at(2 * pair + 1, 2),
            )
            for slot in range(slots):
                value = value + spread[slot] * mask[pl.ds(slot, 1), here]
            finish(pair, here, value)
            return carry

        lax.fori_loop(0, pairs, finish_body, 0)

    def first_finish(pair, here, value):
        new = ((value - center_value * x0[:, here].astype(f32)) / half_width).astype(bf16)
        step_one[:, here] = new
        keep_blocks(pair, new.astype(f32))

    def second_finish(pair, here, value):
        old = step_one[:, here].astype(f32)
        new = (2.0 * (value - center_value * old) / half_width - x0[:, here].astype(f32)).astype(bf16)
        stacked[pl.ds(0, cols), here] = new
        gathered[mine, :, here] = new
        filtered[:, here] = new
        keep_blocks(pair, new.astype(f32))

    def third_finish(pair, here, value):
        stacked[pl.ds(cols, cols), here] = value.astype(bf16)

    def col_copy(slot, peer):
        return pltpu.make_async_remote_copy(
            src_ref=gathered.at[mine],
            dst_ref=gathered.at[slot],
            send_sem=col_send.at[peer],
            recv_sem=col_recv.at[slot],
            device_id={"col": peer},
            device_id_type=MESH,
        )

    apply_operator(0, x0, first_finish)
    apply_operator(1, step_one, second_finish)
    for step in range(1, n_col):
        peer = lax.rem(mine + step, n_col)
        col_copy(mine, peer).start()
    apply_operator(2, stacked.at[pl.ds(0, cols)], third_finish)
    for step in range(1, n_col):
        peer = lax.rem(mine + step, n_col)
        col_copy(peer, peer).wait_recv()

    piece = 2 * cols // n_row
    part = dot(stacked[...], gathered[...].reshape(n_col * cols, length), NT)
    for at in range(n_row):
        piece_out[at] = part[at * piece : (at + 1) * piece].astype(piece_out.dtype)

    def piece_copy(slot_here, slot_there, peer):
        return pltpu.make_async_remote_copy(
            src_ref=piece_out.at[slot_here],
            dst_ref=piece_in.at[slot_there],
            send_sem=piece_send.at[slot_here],
            recv_sem=piece_recv.at[slot_there],
            device_id={"row": peer},
            device_id_type=MESH,
        )

    def sum_copy(slot_there, peer):
        return pltpu.make_async_remote_copy(
            src_ref=sum_out,
            dst_ref=sum_in.at[slot_there],
            send_sem=sum_send.at[peer],
            recv_sem=sum_recv.at[slot_there],
            device_id={"row": peer},
            device_id_type=MESH,
        )

    peers = [lax.rem(me + step, n_row) for step in range(1, n_row)]
    for peer in peers:
        piece_copy(peer, me, peer).start()
    piece_in[me] = piece_out[me]
    for peer in peers:
        piece_copy(peer, peer, peer).wait_recv()
    summed = piece_in[0].astype(f32)
    for peer in range(1, n_row):
        summed = summed + piece_in[peer].astype(f32)
    sum_out[...] = summed.astype(sum_out.dtype)
    for peer in peers:
        sum_copy(me, peer).start()
    sum_in[me] = sum_out[...]
    for peer in peers:
        sum_copy(peer, peer).wait_recv()
    for peer in peers:
        for phase in range(3):
            row_copy(phase, peer, me, peer).wait_send()
        piece_copy(peer, me, peer).wait_send()
        sum_copy(me, peer).wait_send()
    for step in range(1, n_col):
        peer = lax.rem(mine + step, n_col)
        col_copy(mine, peer).wait_send()


def on_device(vectors, hblocks, counts, sources, send_rows):
    rows = hblocks.shape[0]
    cols, length = vectors.shape
    slots = send_rows.shape[0]
    n_row = lax.axis_size("row")
    n_col = lax.axis_size("col")
    assert slots == 2 * n_row
    named = rows + slots
    tiles = length // TILE
    total_cols = n_col * cols
    piece = 2 * cols // n_row
    sum_type = jnp.bfloat16 if piece % 16 == 0 else jnp.float32
    smem = pl.BlockSpec(memory_space=pltpu.SMEM)
    vmem = pl.BlockSpec(memory_space=pltpu.VMEM)
    dma = pltpu.SemaphoreType.DMA
    bf16 = jnp.bfloat16
    f32 = jnp.float32
    by_slot = sources.T
    dense, diagonal, holder = pl.pallas_call(
        functools.partial(build_kernel, rows, slots),
        grid=(K + tiles,),
        out_shape=(
            jax.ShapeDtypeStruct((tiles, length, TILE), bf16),
            jax.ShapeDtypeStruct((slots // 4, TILE, TILE), bf16),
            jax.ShapeDtypeStruct((slots,), jnp.int32),
        ),
        in_specs=[smem, smem, pl.BlockSpec((1, rows, B * B), lambda step: (jnp.minimum(step, K - 1), 0, 0))],
        out_specs=(
            pl.BlockSpec((1, length, TILE), lambda step: (jnp.maximum(step - K, 0), 0, 0)),
            pl.BlockSpec((slots // 4, TILE, TILE), lambda step: (0, 0, 0)),
            smem,
        ),
        scratch_shapes=[
            pltpu.VMEM((TILE, TILE), bf16),
            pltpu.VMEM((TILE, TILE), bf16),
            pltpu.VMEM((HALF * (rows + 8), PAIR), f32),
            pltpu.VMEM((rows, named // 2, B, PAIR), bf16),
        ],
        compiler_params=pltpu.CompilerParams(vmem_limit_bytes=56 * 1024 * 1024),
    )(by_slot, counts, hblocks.transpose(1, 0, 2))

    ordered, sums = pl.pallas_call(
        functools.partial(filter_kernel, n_row, n_col),
        out_shape=(
            jax.ShapeDtypeStruct((cols, length), bf16),
            jax.ShapeDtypeStruct((n_row, piece, total_cols), sum_type),
        ),
        in_specs=[smem, smem, smem, vmem, vmem, pl.BlockSpec(memory_space=pl.ANY)],
        out_specs=(vmem, vmem),
        scratch_shapes=[
            pltpu.VMEM((tiles, length, TILE), bf16),
            pltpu.VMEM((slots, length), f32),
            pltpu.VMEM((cols, length), bf16),
            pltpu.VMEM((cols, length), bf16),
            pltpu.VMEM((2 * cols, length), bf16),
            pltpu.VMEM((cols, length), f32),
            pltpu.VMEM((rows, cols, PAIR), bf16),
            pltpu.VMEM((slots, cols, PAIR), f32),
            pltpu.VMEM((slots + 1, cols, PAIR), f32),
            pltpu.VMEM((3, n_row, cols, 2 * PAIR), bf16),
            pltpu.VMEM((3, n_row, cols, 2 * PAIR), bf16),
            pltpu.VMEM((n_col, cols, length), bf16),
            pltpu.VMEM((n_row, piece, total_cols), sum_type),
            pltpu.VMEM((n_row, piece, total_cols), sum_type),
            pltpu.VMEM((piece, total_cols), sum_type),
            dma((tiles,)),
            dma((3, n_row)), dma((3, n_row)),
            dma((n_col,)), dma((n_col,)),
            dma((n_row,)), dma((n_row,)),
            dma((n_row,)), dma((n_row,)),
        ],
        compiler_params=pltpu.CompilerParams(
            collective_id=0, has_side_effects=True, vmem_limit_bytes=56 * 1024 * 1024
        ),
    )(send_rows, by_slot, holder, vectors, diagonal, dense)

    filtered, gram, projected = pl.pallas_call(
        functools.partial(output_kernel, cols),
        out_shape=(
            jax.ShapeDtypeStruct((cols, length), bf16),
            jax.ShapeDtypeStruct((cols, total_cols), f32),
            jax.ShapeDtypeStruct((cols, total_cols), f32),
        ),
        in_specs=[vmem, vmem],
        out_specs=(vmem, vmem, vmem),
    )(ordered, sums)
    return filtered, gram.T, projected.T


def solution(mesh):
    return jax.shard_map(
        on_device,
        mesh=mesh,
        in_specs=(P("col", "row"), P("row", None, None), P("row"), P("row", None), P("row")),
        out_specs=(P("col", "row"), P(None, "col"), P(None, "col")),
        check_vma=False,
    )
```

time: 83.1 us -> 73.3 us (0.88)
  local copies, waits for them, and re-layouts: 5.55 us -> 0 us
  other arithmetic: 2.85 us -> 0 us
  Pallas kernels: 73.7 us -> 72.5 us
    unnamed x3 -> x0, local copies, waits for them, and re-layouts: 4.61 us -> none
    concatenate x1 -> x0, other arithmetic: 1.25 us -> none  [on_device(): index = jnp.concatenate([send_rows, holder, entry])]
    pallas_call x1 -> x3, Pallas kernels: 73.7 us -> 72.5 us  [the longest x1 47.6 us: on_device(): pl.pallas_call(functools.partial(filter_kernel, n_row, n_col), out_shape=...]
    reshape x4 -> x0, local copies, waits for them, and re-layouts: 0.85 us -> none  [the longest x3 0.75 us: on_device(): key.reshape(rows // GROUP, GROUP, K).transpose(0, 2, 1)]
where the time goes in v2:
time: 73.3 us; the launch traced here: 73.1 us
  Pallas kernels  72.5 us (99%)
    pallas_call x1, Pallas kernels, on_device(): pl.pallas_call(functools.partial(filter_kernel, n_row, n_col), out_shape=...  47.6 us
    pallas_call x1, Pallas kernels, on_device(): pl.pallas_call(functools.partial(build_kernel, rows, slots), grid=(K + ti...  22.8 us
    pallas_call x1, Pallas kernels, on_device(): pl.pallas_call(functools.partial(output_kernel, cols), out_shape=(jax.Sha...  2.1 us

profile of v2, /device:TPU:1, one launch (start us, length us, event | category | flops | bytes accessed | tf_op | source)
XLA Modules:
  0.0 73.1 jit_solution(291747909403620826)
XLA Ops:
  0.6 22.8 %shard_map.76 = (bf16[8,2048,256]{2,1,0:T(8,128)(2,1)}, bf16[4,256,256]{2,1,0:T(8,128)(2,1)}, s32[16]{0:T(128)}) custom-call(s32[12,32]{1,0:T(8,128)} %bitcast.5, s32[32]{0:T(128)} %counts.1, bf16[12,32,4096]{2,1,0:T(8,128)(2,1)} %bitcast.4), custom_call_target="tpu_custom_call" | custom-call | tf_op jit(solution)/shard_map/pallas_call | solution.py:382
  23.4 47.6 %shard_map.77 = (bf16[64,2048]{1,0:T(8,128)(2,1)}, bf16[8,16,256]{2,1,0:T(8,128)(2,1)}) custom-call(s32[16]{0:T(128)} %send_rows.1, s32[12,32]{1,0:T(8,128)} %bitcast.6, s32[16]{0:T(128)} %get-tuple-element.11.holder, bf16[64,2048]{1,0:T(8,128)(2,1)} %x_in.1, bf16[4,256,256]{2,1,0:T(8,128)(2,1)} %get-tuple-element.12.diagonal, ...), custom_call_target="tpu_custom_call" | custom-call | tf_op jit(solution)/shard_map/pallas_call | solution.py:405
  71.0 2.1 %shard_map.78 = (bf16[64,2048]{1,0:T(8,128)(2,1)}, f32[64,256]{1,0:T(8,128)}, f32[64,256]{1,0:T(8,128)}) custom-call(bf16[64,2048]{1,0:T(8,128)(2,1)} %get-tuple-element.14.ordered, bf16[8,16,256]{2,1,0:T(8,128)(2,1)} %get-tuple-element.15.sums), custom_call_target="tpu_custom_call" | custom-call | tf_op jit(solution)/shard_map/pallas_call | solution.py:440

commit v3 on v2

--- a/solution.py
+++ b/solution.py
@@ -11,7 +11,9 @@
 K = 12
 PAIR = 2 * B
 TILE = 256
-UNROLL = 4
+UNROLL = 8
+SLOTS_STEP = 3
+TILES_STEP = 2
 HALF = B // 2
 
 center_value = 0.25
@@ -26,24 +28,28 @@
     return lax.dot_general(a, b, dims, preferred_element_type=jnp.float32)
 
 
-def order_matrix():
+def order_matrix(turned=0):
     row_at = lax.broadcasted_iota(jnp.int32, (TILE, TILE), 0)
     col_at = lax.broadcasted_iota(jnp.int32, (TILE, TILE), 1)
     within = row_at & (B - 1)
     target = (row_at - within) + (within & 1) * HALF + (within >> 1)
+    target = target ^ turned
     return jnp.where(target == col_at, 1.0, 0.0).astype(jnp.bfloat16)
 
 
-def build_kernel(rows, slots, sources, counts, h, dense, diagonal, holder, order, ident, placed, upper):
+def build_kernel(rows, slots, sources, counts, h, dense, diagonal, holder, order, order_turned, ident, placed, upper):
     step = pl.program_id(0)
     per_tile = TILE // B
     tiles = rows // per_tile
     stride = rows + 8
+    size = HALF * stride
+    place_steps = K // SLOTS_STEP
     bf16 = jnp.bfloat16
 
     @pl.when(step == 0)
     def _():
         order[...] = order_matrix()
+        order_turned[...] = order_matrix(B)
         row_at = lax.broadcasted_iota(jnp.int32, (TILE, TILE), 0)
         col_at = lax.broadcasted_iota(jnp.int32, (TILE, TILE), 1)
         ident[...] = jnp.where(row_at == col_at, 1.0, 0.0).astype(bf16)
@@ -67,42 +73,47 @@
 
         lax.fori_loop(0, rows, holder_body, 0)
 
-    @pl.when(step < K)
+    @pl.when(step < place_steps)
     def _():
         pieces = B * B // TILE
-        lanes = jnp.concatenate([h[0, :, at * TILE : (at + 1) * TILE] for at in range(pieces)], 0)
-        value = dot(lanes, order[...], NN)
-        for at in range(pieces):
-            part = value[at * rows : (at + 1) * rows]
-            placed[pl.ds(2 * at * stride, rows), :] = part[:, :PAIR]
-            placed[pl.ds((2 * at + 1) * stride, rows), :] = part[:, PAIR:]
         side = lax.broadcasted_iota(jnp.int32, (HALF, PAIR), 1) >> 6
 
-        def add_body(group, carry):
-            news = []
-            for inner in range(UNROLL):
-                row = group * UNROLL + inner
-                source = sources[step, row]
-                half = source & 1
-                wanted = jnp.where(step < counts[row], half, 2)
-                straight = placed[pl.ds(row, HALF, stride=stride), :]
-                turned = pltpu.roll(straight, B, 1)
-                keep = side == wanted
-                first = jnp.broadcast_to(half, (HALF, PAIR)) == 0
-                even = jnp.where(keep, jnp.where(first, straight, turned), 0.0)
-                odd = jnp.where(keep, jnp.where(first, turned, straight), 0.0)
-                old = upper[row, source >> 1]
-                news.append((row, source >> 1, old + jnp.concatenate([even, odd], 0).astype(bf16)))
-            for row, pair, new in news:
-                upper[row, pair] = new
-            return carry
-
-        lax.fori_loop(0, rows // UNROLL, add_body, 0)
-
-    @pl.when(step >= K)
+        def slot_body(inner_slot, carry):
+            slot = step * SLOTS_STEP + inner_slot
+            lanes = jnp.concatenate([h[inner_slot, :, at * TILE : (at + 1) * TILE] for at in range(pieces)], 0)
+            for turned, matrix in enumerate((order, order_turned)):
+                value = dot(lanes, matrix[...], NN)
+                for at in range(pieces):
+                    part = value[at * rows : (at + 1) * rows]
+                    placed[pl.ds(turned * size + 2 * at * stride, rows), :] = part[:, :PAIR]
+                    placed[pl.ds(turned * size + (2 * at + 1) * stride, rows), :] = part[:, PAIR:]
+
+            def add_body(group, carry):
+                news = []
+                for inner in range(UNROLL):
+                    row = group * UNROLL + inner
+                    source = sources[slot, row]
+                    half = source & 1
+                    keep = side == jnp.where(slot < counts[row], half, 2)
+                    even = placed[pl.ds(half * size + row, HALF, stride=stride), :]
+                    odd = placed[pl.ds((1 - half) * size + row, HALF, stride=stride), :]
+                    even = jnp.where(keep, even, 0.0).astype(bf16)
+                    odd = jnp.where(keep, odd, 0.0).astype(bf16)
+                    old = upper[row, source >> 1]
+                    news.append((row, source >> 1, old + jnp.concatenate([even, odd], 0)))
+                for row, pair, new in news:
+                    upper[row, pair] = new
+                return carry
+
+            return lax.fori_loop(0, rows // UNROLL, add_body, carry)
+
+        lax.fori_loop(0, SLOTS_STEP, slot_body, 0)
+
+    @pl.when(step >= place_steps)
     def _():
-        tile = step - K
-        for other in range(tiles):
+        for inner, other in [(inner, other) for inner in range(TILES_STEP) for other in range(tiles)]:
+            tile = (step - place_steps) * TILES_STEP + inner
+
             def block(at_row, at_col):
                 return jnp.concatenate(
                     [
@@ -113,9 +124,9 @@
                 )
 
             value = dot(ident[...], block(tile, other), NT) + block(other, tile).astype(jnp.float32)
-            dense[0, pl.ds(other * TILE, TILE), :] = value.astype(bf16)
-
-    @pl.when(step == K + tiles - 1)
+            dense[inner, pl.ds(other * TILE, TILE), :] = value.astype(bf16)
+
+    @pl.when(step == pl.num_programs(0) - 1)
     def _():
         low = lax.broadcasted_iota(jnp.int32, (B, PAIR), 1) < B
         for slot in range(slots):
@@ -224,7 +235,7 @@
     def pick(first, second):
         return jnp.where(low, blocks[first].astype(f32), blocks[second].astype(f32)).astype(bf16)
 
-    def apply_operator(phase, source, finish):
+    def apply_operator(phase, source, finish, beside=None):
         for pack in range(slots // 4):
             at = 4 * pack
             near = jnp.concatenate([pick(holder[at], holder[at + 1]), pick(holder[at + 2], holder[at + 3])], 1)
@@ -248,6 +259,8 @@
         for step in range(1, n_row):
             peer = lax.rem(me + step, n_row)
             row_copy(phase, peer, peer, peer).wait_recv()
+        if beside is not None:
+            beside()
 
         for pack in range(slots // 4):
             far = jnp.concatenate([in_buf[phase, 2 * pack + inner, :, pl.ds(0, PAIR)] for inner in range(2)], 1)
@@ -291,25 +304,40 @@
     def third_finish(pair, here, value):
         stacked[pl.ds(cols, cols), here] = value.astype(bf16)
 
-    def col_copy(slot, peer):
+    def col_copy(slot_here, slot_there, sem_at, peer):
         return pltpu.make_async_remote_copy(
-            src_ref=gathered.at[mine],
-            dst_ref=gathered.at[slot],
-            send_sem=col_send.at[peer],
-            recv_sem=col_recv.at[slot],
+            src_ref=gathered.at[slot_here],
+            dst_ref=gathered.at[slot_there],
+            send_sem=col_send.at[sem_at],
+            recv_sem=col_recv.at[slot_there],
             device_id={"col": peer},
             device_id_type=MESH,
         )
 
+    sibling = mine + 1 - 2 * lax.rem(mine, 2)
+    across = [lax.rem(mine + 2 * step, n_col) for step in range(1, n_col // 2)]
+
+    def start_gather():
+        for at, peer in enumerate(across):
+            col_copy(mine, mine, at, peer).start()
+        col_copy(mine, mine, len(across), sibling).start()
+
+    def forward_gather():
+        for at, peer in enumerate(across):
+            col_copy(peer, peer, at, peer).wait_recv()
+            col_copy(peer, peer, len(across) + 1 + at, sibling).start()
+
+    def end_gather():
+        col_copy(sibling, sibling, 0, sibling).wait_recv()
+        for peer in across:
+            other = peer + 1 - 2 * lax.rem(peer, 2)
+            col_copy(other, other, 0, sibling).wait_recv()
+
     apply_operator(0, x0, first_finish)
     apply_operator(1, step_one, second_finish)
-    for step in range(1, n_col):
-        peer = lax.rem(mine + step, n_col)
-        col_copy(mine, peer).start()
-    apply_operator(2, stacked.at[pl.ds(0, cols)], third_finish)
-    for step in range(1, n_col):
-        peer = lax.rem(mine + step, n_col)
-        col_copy(peer, peer).wait_recv()
+    start_gather()
+    apply_operator(2, stacked.at[pl.ds(0, cols)], third_finish, forward_gather)
+    end_gather()
 
     piece = 2 * cols // n_row
     part = dot(stacked[...], gathered[...].reshape(n_col * cols, length), NT)
@@ -356,9 +384,10 @@
             row_copy(phase, peer, me, peer).wait_send()
         piece_copy(peer, me, peer).wait_send()
         sum_copy(me, peer).wait_send()
-    for step in range(1, n_col):
-        peer = lax.rem(mine + step, n_col)
-        col_copy(mine, peer).wait_send()
+    for at, peer in enumerate(across):
+        col_copy(mine, mine, at, peer).wait_send()
+        col_copy(peer, peer, len(across) + 1 + at, sibling).wait_send()
+    col_copy(mine, mine, len(across), sibling).wait_send()
 
 
 def on_device(vectors, hblocks, counts, sources, send_rows):
@@ -379,24 +408,26 @@
     bf16 = jnp.bfloat16
     f32 = jnp.float32
     by_slot = sources.T
+    place_steps = K // SLOTS_STEP
     dense, diagonal, holder = pl.pallas_call(
         functools.partial(build_kernel, rows, slots),
-        grid=(K + tiles,),
+        grid=(place_steps + tiles // TILES_STEP,),
         out_shape=(
             jax.ShapeDtypeStruct((tiles, length, TILE), bf16),
             jax.ShapeDtypeStruct((slots // 4, TILE, TILE), bf16),
             jax.ShapeDtypeStruct((slots,), jnp.int32),
         ),
-        in_specs=[smem, smem, pl.BlockSpec((1, rows, B * B), lambda step: (jnp.minimum(step, K - 1), 0, 0))],
+        in_specs=[smem, smem, pl.BlockSpec((SLOTS_STEP, rows, B * B), lambda step: (jnp.minimum(step, place_steps - 1), 0, 0))],
         out_specs=(
-            pl.BlockSpec((1, length, TILE), lambda step: (jnp.maximum(step - K, 0), 0, 0)),
+            pl.BlockSpec((TILES_STEP, length, TILE), lambda step: (jnp.maximum(step - place_steps, 0), 0, 0)),
             pl.BlockSpec((slots // 4, TILE, TILE), lambda step: (0, 0, 0)),
             smem,
         ),
         scratch_shapes=[
             pltpu.VMEM((TILE, TILE), bf16),
             pltpu.VMEM((TILE, TILE), bf16),
-            pltpu.VMEM((HALF * (rows + 8), PAIR), f32),
+            pltpu.VMEM((TILE, TILE), bf16),
+            pltpu.VMEM((2 * HALF * (rows + 8), PAIR), f32),
             pltpu.VMEM((rows, named // 2, B, PAIR), bf16),
         ],
         compiler_params=pltpu.CompilerParams(vmem_limit_bytes=56 * 1024 * 1024),

time: 73.3 us -> 65.7 us (0.90)
  the two profiles are of different devices: /device:TPU:1 before, /device:TPU:0 now
where the time goes in v3:
time: 65.7 us; the launch traced here: 65.5 us
  Pallas kernels  64.9 us (99%)
    pallas_call x1, Pallas kernels, on_device(): pl.pallas_call(functools.partial(filter_kernel, n_row, n_col), out_shape=...  45.8 us
    pallas_call x1, Pallas kernels, on_device(): pl.pallas_call(functools.partial(build_kernel, rows, slots), grid=(place_...  16.9 us
    pallas_call x1, Pallas kernels, on_device(): pl.pallas_call(functools.partial(output_kernel, cols), out_shape=(jax.Sha...  2.11 us

profile of v3, /device:TPU:0, one launch (start us, length us, event | category | flops | bytes accessed | tf_op | source)
XLA Modules:
  0.0 65.5 jit_solution(3671049502942703638)
XLA Ops:
  0.6 16.9 %shard_map.76 = (bf16[8,2048,256]{2,1,0:T(8,128)(2,1)}, bf16[4,256,256]{2,1,0:T(8,128)(2,1)}, s32[16]{0:T(128)}) custom-call(s32[12,32]{1,0:T(8,128)} %bitcast.5, s32[32]{0:T(128)} %counts.1, bf16[12,32,4096]{2,1,0:T(8,128)(2,1)} %bitcast.4), custom_call_target="tpu_custom_call" | custom-call | tf_op jit(solution)/shard_map/pallas_call | solution.py:412
  17.6 45.8 %shard_map.77 = (bf16[64,2048]{1,0:T(8,128)(2,1)}, bf16[8,16,256]{2,1,0:T(8,128)(2,1)}) custom-call(s32[16]{0:T(128)} %send_rows.1, s32[12,32]{1,0:T(8,128)} %bitcast.6, s32[16]{0:T(128)} %get-tuple-element.11.holder, bf16[64,2048]{1,0:T(8,128)(2,1)} %x_in.1, bf16[4,256,256]{2,1,0:T(8,128)(2,1)} %get-tuple-element.12.diagonal, ...), custom_call_target="tpu_custom_call" | custom-call | tf_op jit(solution)/shard_map/pallas_call | solution.py:436
  63.4 2.1 %shard_map.78 = (bf16[64,2048]{1,0:T(8,128)(2,1)}, f32[64,256]{1,0:T(8,128)}, f32[64,256]{1,0:T(8,128)}) custom-call(bf16[64,2048]{1,0:T(8,128)(2,1)} %get-tuple-element.14.ordered, bf16[8,16,256]{2,1,0:T(8,128)(2,1)} %get-tuple-element.15.sums), custom_call_target="tpu_custom_call" | custom-call | tf_op jit(solution)/shard_map/pallas_call | solution.py:471

commit v4 on v3

--- a/solution.py
+++ b/solution.py
@@ -12,8 +12,7 @@
 PAIR = 2 * B
 TILE = 256
 UNROLL = 8
-SLOTS_STEP = 3
-TILES_STEP = 2
+ROWS_STEP = 16
 HALF = B // 2
 
 center_value = 0.25
@@ -37,105 +36,79 @@
     return jnp.where(target == col_at, 1.0, 0.0).astype(jnp.bfloat16)
 
 
-def build_kernel(rows, slots, sources, counts, h, dense, diagonal, holder, order, order_turned, ident, placed, upper):
+def build_kernel(rows, sources, counts, h, upper, diagonal, holder, order, order_turned, placed, remote):
     step = pl.program_id(0)
-    per_tile = TILE // B
-    tiles = rows // per_tile
-    stride = rows + 8
+    here = upper.shape[0]
+    slots = remote.shape[0]
+    stride = here + 8
     size = HALF * stride
-    place_steps = K // SLOTS_STEP
+    first_row = step * here
     bf16 = jnp.bfloat16
 
     @pl.when(step == 0)
     def _():
         order[...] = order_matrix()
         order_turned[...] = order_matrix(B)
-        row_at = lax.broadcasted_iota(jnp.int32, (TILE, TILE), 0)
-        col_at = lax.broadcasted_iota(jnp.int32, (TILE, TILE), 1)
-        ident[...] = jnp.where(row_at == col_at, 1.0, 0.0).astype(bf16)
-        diagonal[...] = jnp.zeros_like(diagonal)
-
-        def clear_body(row, carry):
-            upper[row] = jnp.zeros_like(upper[row])
+
+    def clear_body(row, carry):
+        upper[row] = jnp.zeros_like(upper[row])
+        return carry
+
+    lax.fori_loop(0, here, clear_body, 0)
+    pieces = B * B // TILE
+    side = lax.broadcasted_iota(jnp.int32, (HALF, PAIR), 1) >> 6
+
+    def slot_body(slot, carry):
+        lanes = jnp.concatenate([h[slot, :, at * TILE : (at + 1) * TILE] for at in range(pieces)], 0)
+        for turned, matrix in enumerate((order, order_turned)):
+            value = dot(lanes, matrix[...], NN)
+            for at in range(pieces):
+                part = value[at * here : (at + 1) * here]
+                placed[pl.ds(turned * size + 2 * at * stride, here), :] = part[:, :PAIR]
+                placed[pl.ds(turned * size + (2 * at + 1) * stride, here), :] = part[:, PAIR:]
+
+        def add_body(group, carry):
+            news = []
+            for inner in range(UNROLL):
+                row = group * UNROLL + inner
+                source = sources[slot, first_row + row]
+                half = source & 1
+                keep = side == jnp.where(slot < counts[first_row + row], half, 2)
+                even = placed[pl.ds(half * size + row, HALF, stride=stride), :]
+                odd = placed[pl.ds((1 - half) * size + row, HALF, stride=stride), :]
+                even = jnp.where(keep, even, 0.0).astype(bf16)
+                odd = jnp.where(keep, odd, 0.0).astype(bf16)
+                old = upper[row, source >> 1]
+                news.append((row, source >> 1, old + jnp.concatenate([even, odd], 0)))
+            for row, pair, new in news:
+                upper[row, pair] = new
             return carry
 
-        lax.fori_loop(0, rows, clear_body, 0)
-
-        def holder_body(row, carry):
-            for slot in (1, 2):
-                source = sources[slot, row]
-
-                @pl.when(source >= rows)
-                def _():
-                    holder[source - rows] = row
-
-            return carry
-
-        lax.fori_loop(0, rows, holder_body, 0)
-
-    @pl.when(step < place_steps)
-    def _():
-        pieces = B * B // TILE
-        side = lax.broadcasted_iota(jnp.int32, (HALF, PAIR), 1) >> 6
-
-        def slot_body(inner_slot, carry):
-            slot = step * SLOTS_STEP + inner_slot
-            lanes = jnp.concatenate([h[inner_slot, :, at * TILE : (at + 1) * TILE] for at in range(pieces)], 0)
-            for turned, matrix in enumerate((order, order_turned)):
-                value = dot(lanes, matrix[...], NN)
-                for at in range(pieces):
-                    part = value[at * rows : (at + 1) * rows]
-                    placed[pl.ds(turned * size + 2 * at * stride, rows), :] = part[:, :PAIR]
-                    placed[pl.ds(turned * size + (2 * at + 1) * stride, rows), :] = part[:, PAIR:]
-
-            def add_body(group, carry):
-                news = []
-                for inner in range(UNROLL):
-                    row = group * UNROLL + inner
-                    source = sources[slot, row]
-                    half = source & 1
-                    keep = side == jnp.where(slot < counts[row], half, 2)
-                    even = placed[pl.ds(half * size + row, HALF, stride=stride), :]
-                    odd = placed[pl.ds((1 - half) * size + row, HALF, stride=stride), :]
-                    even = jnp.where(keep, even, 0.0).astype(bf16)
-                    odd = jnp.where(keep, odd, 0.0).astype(bf16)
-                    old = upper[row, source >> 1]
-                    news.append((row, source >> 1, old + jnp.concatenate([even, odd], 0)))
-                for row, pair, new in news:
-                    upper[row, pair] = new
-                return carry
-
-            return lax.fori_loop(0, rows // UNROLL, add_body, carry)
-
-        lax.fori_loop(0, SLOTS_STEP, slot_body, 0)
-
-    @pl.when(step >= place_steps)
-    def _():
-        for inner, other in [(inner, other) for inner in range(TILES_STEP) for other in range(tiles)]:
-            tile = (step - place_steps) * TILES_STEP + inner
-
-            def block(at_row, at_col):
-                return jnp.concatenate(
-                    [
-                        upper[pl.ds(at_row * per_tile, per_tile), 2 * at_col + side].reshape(TILE, PAIR)
-                        for side in range(2)
-                    ],
-                    1,
-                )
-
-            value = dot(ident[...], block(tile, other), NT) + block(other, tile).astype(jnp.float32)
-            dense[inner, pl.ds(other * TILE, TILE), :] = value.astype(bf16)
+        return lax.fori_loop(0, here // UNROLL, add_body, carry)
+
+    lax.fori_loop(0, K, slot_body, 0)
+    block_side = lax.broadcasted_iota(jnp.int32, (B, PAIR), 1) >> 6
+
+    def remote_body(row, carry):
+        for slot in (1, 2):
+            source = sources[slot, first_row + row]
+
+            @pl.when(source >= rows)
+            def _():
+                holder[source - rows] = first_row + row
+                value = upper[row, source >> 1].astype(jnp.float32)
+                remote[source - rows] = jnp.where(block_side == (source & 1), value, 0.0).astype(bf16)
+
+        return carry
+
+    lax.fori_loop(0, here, remote_body, 0)
 
     @pl.when(step == pl.num_programs(0) - 1)
     def _():
-        low = lax.broadcasted_iota(jnp.int32, (B, PAIR), 1) < B
+        diagonal[...] = jnp.zeros_like(diagonal)
         for slot in range(slots):
-            value = upper[holder[slot], (rows + slot) // 2].astype(jnp.float32)
-            keep = low if slot % 2 == 0 else jnp.logical_not(low)
             part = slot % 4
-            diagonal[slot // 4, pl.ds(part * B, B), pl.ds((part // 2) * PAIR, PAIR)] = jnp.where(
-                keep, value, 0.0
-            ).astype(bf16)
+            diagonal[slot // 4, pl.ds(part * B, B), pl.ds((part // 2) * PAIR, PAIR)] = remote[slot]
 
 
 def output_kernel(cols, ordered, sums, filtered, gram, projected):
@@ -169,6 +142,7 @@
     pairs = length // PAIR
     slots = 2 * n_row
     tiles = length // TILE
+    per_tile = TILE // B
     bf16 = jnp.bfloat16
     f32 = jnp.float32
 
@@ -179,7 +153,10 @@
         pl.semaphore_signal(barrier, inc=1, device_id={"col": lax.rem(mine + step, n_col)}, device_id_type=MESH)
 
     def dense_copy(tile):
-        return pltpu.make_async_copy(dense_in.at[tile], dense.at[tile], dense_sem.at[tile])
+        here = pl.ds(tile * per_tile, per_tile)
+        return pltpu.make_async_copy(
+            dense_in.at[here, pl.ds(0, pairs)], dense.at[here], dense_sem.at[tile]
+        )
 
     for tile in range(tiles):
         dense_copy(tile).start()
@@ -250,10 +227,16 @@
         in_buf[phase, me] = out_buf[phase, me]
 
         def local_body(tile, carry):
-            if phase == 0:
+            down = jnp.concatenate([dense[:, 2 * tile + side].reshape(length, PAIR) for side in range(2)], 1)
+            along = jnp.concatenate(
+                [dense[pl.ds(tile * per_tile, per_tile), pair].reshape(TILE, PAIR) for pair in range(pairs)], 1
+            )
+            total[:, columns(tile, TILE)] = dot(source[...], down, NN) + dot(source[...], along, NT)
+            return carry
+
+        if phase == 0:
+            for tile in range(tiles):
                 dense_copy(tile).wait()
-            total[:, columns(tile, TILE)] = dot(source[...], dense[tile], NN)
-            return carry
 
         lax.fori_loop(0, tiles, local_body, 0)
         for step in range(1, n_row):
@@ -408,27 +391,25 @@
     bf16 = jnp.bfloat16
     f32 = jnp.float32
     by_slot = sources.T
-    place_steps = K // SLOTS_STEP
-    dense, diagonal, holder = pl.pallas_call(
-        functools.partial(build_kernel, rows, slots),
-        grid=(place_steps + tiles // TILES_STEP,),
+    upper, diagonal, holder = pl.pallas_call(
+        functools.partial(build_kernel, rows),
+        grid=(rows // ROWS_STEP,),
         out_shape=(
-            jax.ShapeDtypeStruct((tiles, length, TILE), bf16),
+            jax.ShapeDtypeStruct((rows, named // 2, B, PAIR), bf16),
             jax.ShapeDtypeStruct((slots // 4, TILE, TILE), bf16),
             jax.ShapeDtypeStruct((slots,), jnp.int32),
         ),
-        in_specs=[smem, smem, pl.BlockSpec((SLOTS_STEP, rows, B * B), lambda step: (jnp.minimum(step, place_steps - 1), 0, 0))],
+        in_specs=[smem, smem, pl.BlockSpec((K, ROWS_STEP, B * B), lambda step: (0, step, 0))],
         out_specs=(
-            pl.BlockSpec((TILES_STEP, length, TILE), lambda step: (jnp.maximum(step - place_steps, 0), 0, 0)),
+            pl.BlockSpec((ROWS_STEP, named // 2, B, PAIR), lambda step: (step, 0, 0, 0)),
             pl.BlockSpec((slots // 4, TILE, TILE), lambda step: (0, 0, 0)),
             smem,
         ),
         scratch_shapes=[
             pltpu.VMEM((TILE, TILE), bf16),
             pltpu.VMEM((TILE, TILE), bf16),
-            pltpu.VMEM((TILE, TILE), bf16),
-            pltpu.VMEM((2 * HALF * (rows + 8), PAIR), f32),
-            pltpu.VMEM((rows, named // 2, B, PAIR), bf16),
+            pltpu.VMEM((2 * HALF * (ROWS_STEP + 8), PAIR), f32),
+            pltpu.VMEM((slots, B, PAIR), bf16),
         ],
         compiler_params=pltpu.CompilerParams(vmem_limit_bytes=56 * 1024 * 1024),
     )(by_slot, counts, hblocks.transpose(1, 0, 2))
@@ -442,7 +423,7 @@
         in_specs=[smem, smem, smem, vmem, vmem, pl.BlockSpec(memory_space=pl.ANY)],
         out_specs=(vmem, vmem),
         scratch_shapes=[
-            pltpu.VMEM((tiles, length, TILE), bf16),
+            pltpu.VMEM((rows, length // PAIR, B, PAIR), bf16),
             pltpu.VMEM((slots, length), f32),
             pltpu.VMEM((cols, length), bf16),
             pltpu.VMEM((cols, length), bf16),
@@ -466,7 +447,7 @@
         compiler_params=pltpu.CompilerParams(
             collective_id=0, has_side_effects=True, vmem_limit_bytes=56 * 1024 * 1024
         ),
-    )(send_rows, by_slot, holder, vectors, diagonal, dense)
+    )(send_rows, by_slot, holder, vectors, diagonal, upper)
 
     filtered, gram, projected = pl.pallas_call(
         functools.partial(output_kernel, cols),

time: 65.7 us -> 65.6 us (level)
  no operation moved by 1% of the time
where the time goes in v4:
time: 65.6 us; the launch traced here: 65.4 us
  Pallas kernels  64.7 us (99%)
    pallas_call x1, Pallas kernels, on_device(): pl.pallas_call(functools.partial(filter_kernel, n_row, n_col), out_shape=...  45.8 us
    pallas_call x1, Pallas kernels, on_device(): pl.pallas_call(functools.partial(build_kernel, rows), grid=(rows // ROWS_...  16.8 us
    pallas_call x1, Pallas kernels, on_device(): pl.pallas_call(functools.partial(output_kernel, cols), out_shape=(jax.Sha...  2.1 us

profile of v4, /device:TPU:0, one launch (start us, length us, event | category | flops | bytes accessed | tf_op | source)
XLA Modules:
  0.0 65.4 jit_solution(7839296617723865401)
XLA Ops:
  0.6 16.8 %shard_map.76 = (bf16[32,24,64,128]{3,2,1,0:T(8,128)(2,1)}, bf16[4,256,256]{2,1,0:T(8,128)(2,1)}, s32[16]{0:T(128)}) custom-call(s32[12,32]{1,0:T(8,128)} %bitcast.5, s32[32]{0:T(128)} %counts.1, bf16[12,32,4096]{2,1,0:T(8,128)(2,1)} %bitcast.4), custom_call_target="tpu_custom_call" | custom-call | tf_op jit(solution)/shard_map/pallas_call | solution.py:394
  17.4 45.8 %shard_map.77 = (bf16[64,2048]{1,0:T(8,128)(2,1)}, bf16[8,16,256]{2,1,0:T(8,128)(2,1)}) custom-call(s32[16]{0:T(128)} %send_rows.1, s32[12,32]{1,0:T(8,128)} %bitcast.6, s32[16]{0:T(128)} %get-tuple-element.11.holder, bf16[64,2048]{1,0:T(8,128)(2,1)} %x_in.1, bf16[4,256,256]{2,1,0:T(8,128)(2,1)} %get-tuple-element.12.diagonal, ...), custom_call_target="tpu_custom_call" | custom-call | tf_op jit(solution)/shard_map/pallas_call | solution.py:417
  63.3 2.1 %shard_map.78 = (bf16[64,2048]{1,0:T(8,128)(2,1)}, f32[64,256]{1,0:T(8,128)}, f32[64,256]{1,0:T(8,128)}) custom-call(bf16[64,2048]{1,0:T(8,128)(2,1)} %get-tuple-element.14.ordered, bf16[8,16,256]{2,1,0:T(8,128)(2,1)} %get-tuple-element.15.sums), custom_call_target="tpu_custom_call" | custom-call | tf_op jit(solution)/shard_map/pallas_call | solution.py:452

commit v5 on v4

--- a/solution.py
+++ b/solution.py
@@ -31,62 +31,69 @@
     row_at = lax.broadcasted_iota(jnp.int32, (TILE, TILE), 0)
     col_at = lax.broadcasted_iota(jnp.int32, (TILE, TILE), 1)
     within = row_at & (B - 1)
-    target = (row_at - within) + (within & 1) * HALF + (within >> 1)
+    target = (row_at - within) + (within & 1) * HALF + ((within >> 1) & 1) * (HALF // 2) + (within >> 2)
     target = target ^ turned
     return jnp.where(target == col_at, 1.0, 0.0).astype(jnp.bfloat16)
 
 
-def build_kernel(rows, sources, counts, h, upper, diagonal, holder, order, order_turned, placed, remote):
+def build_kernel(rows, sources, counts, h, upper, diagonal, holder, order, swap, marks, placed, remote):
     step = pl.program_id(0)
     here = upper.shape[0]
     slots = remote.shape[0]
-    stride = here + 8
-    size = HALF * stride
+    pieces = B * B // TILE
     first_row = step * here
     bf16 = jnp.bfloat16
 
     @pl.when(step == 0)
     def _():
-        order[...] = order_matrix()
-        order_turned[...] = order_matrix(B)
+        order[:, pl.ds(0, TILE)] = order_matrix()
+        order[:, pl.ds(TILE, TILE)] = order_matrix(B)
+        row_at = lax.broadcasted_iota(jnp.int32, (TILE, TILE), 0)
+        col_at = lax.broadcasted_iota(jnp.int32, (TILE, TILE), 1)
+        swap[...] = jnp.where(col_at == (row_at & (pieces - 1)) * here + (row_at >> 4), 1.0, 0.0).astype(bf16)
+        side = lax.broadcasted_iota(jnp.int32, (here, PAIR), 1) >> 6
+        for wanted in range(3):
+            marks[wanted] = jnp.where(side == wanted, 1.0, 0.0).astype(bf16)
 
     def clear_body(row, carry):
         upper[row] = jnp.zeros_like(upper[row])
         return carry
 
     lax.fori_loop(0, here, clear_body, 0)
-    pieces = B * B // TILE
-    side = lax.broadcasted_iota(jnp.int32, (HALF, PAIR), 1) >> 6
-
-    def slot_body(slot, carry):
-        lanes = jnp.concatenate([h[slot, :, at * TILE : (at + 1) * TILE] for at in range(pieces)], 0)
-        for turned, matrix in enumerate((order, order_turned)):
-            value = dot(lanes, matrix[...], NN)
-            for at in range(pieces):
-                part = value[at * here : (at + 1) * here]
-                placed[pl.ds(turned * size + 2 * at * stride, here), :] = part[:, :PAIR]
-                placed[pl.ds(turned * size + (2 * at + 1) * stride, here), :] = part[:, PAIR:]
-
-        def add_body(group, carry):
+
+    def order_body(pack, carry):
+        for inner in range(2):
+            slot = 2 * pack + inner
+            lanes = jnp.concatenate([h[slot, :, at * TILE : (at + 1) * TILE] for at in range(pieces)], 0)
+            swapped = dot(swap[...], lanes, NN).astype(bf16)
+            value = dot(swapped, order[...], NN).astype(bf16)
+            for turned in range(2):
+                for part in range(2):
+                    at = (2 * turned + part) * PAIR
+                    placed[slot, turned, part] = value[:, at : at + PAIR].reshape(here, pieces, PAIR)
+        return carry
+
+    lax.fori_loop(0, K // 2, order_body, 0)
+
+    def add_body(slot, carry):
+        for group in range(here // UNROLL):
             news = []
-            for inner in range(UNROLL):
-                row = group * UNROLL + inner
+            for row in range(group * UNROLL, (group + 1) * UNROLL):
                 source = sources[slot, first_row + row]
                 half = source & 1
-                keep = side == jnp.where(slot < counts[first_row + row], half, 2)
-                even = placed[pl.ds(half * size + row, HALF, stride=stride), :]
-                odd = placed[pl.ds((1 - half) * size + row, HALF, stride=stride), :]
-                even = jnp.where(keep, even, 0.0).astype(bf16)
-                odd = jnp.where(keep, odd, 0.0).astype(bf16)
+                mark = marks[jnp.where(slot < counts[first_row + row], half, 2)]
+                blocks = [
+                    placed[slot, turned, part, row] * mark
+                    for turned in (half, 1 - half)
+                    for part in range(2)
+                ]
                 old = upper[row, source >> 1]
-                news.append((row, source >> 1, old + jnp.concatenate([even, odd], 0)))
+                news.append((row, source >> 1, old + jnp.concatenate(blocks, 0)))
             for row, pair, new in news:
                 upper[row, pair] = new
-            return carry
-
-        return lax.fori_loop(0, here // UNROLL, add_body, carry)
-
-    lax.fori_loop(0, K, slot_body, 0)
+        return carry
+
+    lax.fori_loop(0, K, add_body, 0)
     block_side = lax.broadcasted_iota(jnp.int32, (B, PAIR), 1) >> 6
 
     def remote_body(row, carry):
@@ -406,9 +413,10 @@
             smem,
         ),
         scratch_shapes=[
+            pltpu.VMEM((TILE, 2 * TILE), bf16),
             pltpu.VMEM((TILE, TILE), bf16),
-            pltpu.VMEM((TILE, TILE), bf16),
-            pltpu.VMEM((2 * HALF * (ROWS_STEP + 8), PAIR), f32),
+            pltpu.VMEM((3, ROWS_STEP, PAIR), bf16),
+            pltpu.VMEM((K, 2, 2, ROWS_STEP, B * B // TILE, PAIR), bf16),
             pltpu.VMEM((slots, B, PAIR), bf16),
         ],
         compiler_params=pltpu.CompilerParams(vmem_limit_bytes=56 * 1024 * 1024),

time: 65.6 us -> 66.1 us (level)
  no operation moved by 1% of the time
where the time goes in v5:
time: 66.1 us; the launch traced here: 65.9 us
  Pallas kernels  65.3 us (99%)
    pallas_call x1, Pallas kernels, on_device(): pl.pallas_call(functools.partial(filter_kernel, n_row, n_col), out_shape=...  45.8 us
    pallas_call x1, Pallas kernels, on_device(): pl.pallas_call(functools.partial(build_kernel, rows), grid=(rows // ROWS_...  17.3 us
    pallas_call x1, Pallas kernels, on_device(): pl.pallas_call(functools.partial(output_kernel, cols), out_shape=(jax.Sha...  2.11 us

profile of v5, /device:TPU:0, one launch (start us, length us, event | category | flops | bytes accessed | tf_op | source)
XLA Modules:
  0.0 65.9 jit_solution(7021529004929236153)
XLA Ops:
  0.6 17.3 %shard_map.76 = (bf16[32,24,64,128]{3,2,1,0:T(8,128)(2,1)}, bf16[4,256,256]{2,1,0:T(8,128)(2,1)}, s32[16]{0:T(128)}) custom-call(s32[12,32]{1,0:T(8,128)} %bitcast.5, s32[32]{0:T(128)} %counts.1, bf16[12,32,4096]{2,1,0:T(8,128)(2,1)} %bitcast.4), custom_call_target="tpu_custom_call" | custom-call | tf_op jit(solution)/shard_map/pallas_call | solution.py:401
  18.0 45.8 %shard_map.77 = (bf16[64,2048]{1,0:T(8,128)(2,1)}, bf16[8,16,256]{2,1,0:T(8,128)(2,1)}) custom-call(s32[16]{0:T(128)} %send_rows.1, s32[12,32]{1,0:T(8,128)} %bitcast.6, s32[16]{0:T(128)} %get-tuple-element.11.holder, bf16[64,2048]{1,0:T(8,128)(2,1)} %x_in.1, bf16[4,256,256]{2,1,0:T(8,128)(2,1)} %get-tuple-element.12.diagonal, ...), custom_call_target="tpu_custom_call" | custom-call | tf_op jit(solution)/shard_map/pallas_call | solution.py:425
  63.8 2.1 %shard_map.78 = (bf16[64,2048]{1,0:T(8,128)(2,1)}, f32[64,256]{1,0:T(8,128)}, f32[64,256]{1,0:T(8,128)}) custom-call(bf16[64,2048]{1,0:T(8,128)(2,1)} %get-tuple-element.14.ordered, bf16[8,16,256]{2,1,0:T(8,128)(2,1)} %get-tuple-element.15.sums), custom_call_target="tpu_custom_call" | custom-call | tf_op jit(solution)/shard_map/pallas_call | solution.py:460

commit v6 on v5

--- a/solution.py
+++ b/solution.py
@@ -27,27 +27,25 @@
     return lax.dot_general(a, b, dims, preferred_element_type=jnp.float32)
 
 
-def order_matrix(turned=0):
+def order_matrix():
     row_at = lax.broadcasted_iota(jnp.int32, (TILE, TILE), 0)
     col_at = lax.broadcasted_iota(jnp.int32, (TILE, TILE), 1)
     within = row_at & (B - 1)
     target = (row_at - within) + (within & 1) * HALF + ((within >> 1) & 1) * (HALF // 2) + (within >> 2)
-    target = target ^ turned
     return jnp.where(target == col_at, 1.0, 0.0).astype(jnp.bfloat16)
 
 
 def build_kernel(rows, sources, counts, h, upper, diagonal, holder, order, swap, marks, placed, remote):
     step = pl.program_id(0)
     here = upper.shape[0]
-    slots = remote.shape[0]
+    slots = remote.shape[0] - 1
     pieces = B * B // TILE
     first_row = step * here
     bf16 = jnp.bfloat16
 
     @pl.when(step == 0)
     def _():
-        order[:, pl.ds(0, TILE)] = order_matrix()
-        order[:, pl.ds(TILE, TILE)] = order_matrix(B)
+        order[...] = order_matrix()
         row_at = lax.broadcasted_iota(jnp.int32, (TILE, TILE), 0)
         col_at = lax.broadcasted_iota(jnp.int32, (TILE, TILE), 1)
         swap[...] = jnp.where(col_at == (row_at & (pieces - 1)) * here + (row_at >> 4), 1.0, 0.0).astype(bf16)
@@ -66,14 +64,21 @@
             slot = 2 * pack + inner
             lanes = jnp.concatenate([h[slot, :, at * TILE : (at + 1) * TILE] for at in range(pieces)], 0)
             swapped = dot(swap[...], lanes, NN).astype(bf16)
-            value = dot(swapped, order[...], NN).astype(bf16)
-            for turned in range(2):
-                for part in range(2):
-                    at = (2 * turned + part) * PAIR
-                    placed[slot, turned, part] = value[:, at : at + PAIR].reshape(here, pieces, PAIR)
+            value = dot(swapped, order[...], NN)
+            for part in range(2):
+                straight = value[:, part * PAIR : (part + 1) * PAIR]
+                turned = pltpu.roll(straight, B, 1)
+                placed[slot, 0, part] = straight.astype(bf16).reshape(here, pieces, PAIR)
+                placed[slot, 1, part] = turned.astype(bf16).reshape(here, pieces, PAIR)
         return carry
 
     lax.fori_loop(0, K // 2, order_body, 0)
+
+    def marked(slot, row, half, wanted):
+        mark = marks[wanted]
+        return jnp.concatenate(
+            [placed[slot, turned, part, row] * mark for turned in (half, 1 - half) for part in range(2)], 0
+        )
 
     def add_body(slot, carry):
         for group in range(here // UNROLL):
@@ -81,34 +86,32 @@
             for row in range(group * UNROLL, (group + 1) * UNROLL):
                 source = sources[slot, first_row + row]
                 half = source & 1
-                mark = marks[jnp.where(slot < counts[first_row + row], half, 2)]
-                blocks = [
-                    placed[slot, turned, part, row] * mark
-                    for turned in (half, 1 - half)
-                    for part in range(2)
-                ]
-                old = upper[row, source >> 1]
-                news.append((row, source >> 1, old + jnp.concatenate(blocks, 0)))
+                local = source < rows
+                used = jnp.logical_and(slot < counts[first_row + row], local)
+                pair = jnp.where(local, source >> 1, 0)
+                new = upper[row, pair] + marked(slot, row, half, jnp.where(used, half, 2))
+                news.append((row, pair, new))
             for row, pair, new in news:
                 upper[row, pair] = new
         return carry
 
     lax.fori_loop(0, K, add_body, 0)
-    block_side = lax.broadcasted_iota(jnp.int32, (B, PAIR), 1) >> 6
-
-    def remote_body(row, carry):
-        for slot in (1, 2):
-            source = sources[slot, first_row + row]
-
-            @pl.when(source >= rows)
-            def _():
-                holder[source - rows] = first_row + row
-                value = upper[row, source >> 1].astype(jnp.float32)
-                remote[source - rows] = jnp.where(block_side == (source & 1), value, 0.0).astype(bf16)
-
+
+    def remote_body(group, carry):
+        news = []
+        for inner in range(4):
+            row = 4 * group + inner
+            for slot in (1, 2):
+                source = sources[slot, first_row + row]
+                at = jnp.where(source >= rows, source - rows, slots)
+                holder[at] = first_row + row
+                half = source & 1
+                news.append((at, marked(slot, row, half, half)))
+        for at, new in news:
+            remote[at] = new
         return carry
 
-    lax.fori_loop(0, here, remote_body, 0)
+    lax.fori_loop(0, here // 4, remote_body, 0)
 
     @pl.when(step == pl.num_programs(0) - 1)
     def _():
@@ -162,7 +165,7 @@
     def dense_copy(tile):
         here = pl.ds(tile * per_tile, per_tile)
         return pltpu.make_async_copy(
-            dense_in.at[here, pl.ds(0, pairs)], dense.at[here], dense_sem.at[tile]
+            dense_in.at[here], dense.at[here], dense_sem.at[tile]
         )
 
     for tile in range(tiles):
@@ -387,7 +390,6 @@
     n_row = lax.axis_size("row")
     n_col = lax.axis_size("col")
     assert slots == 2 * n_row
-    named = rows + slots
     tiles = length // TILE
     total_cols = n_col * cols
     piece = 2 * cols // n_row
@@ -402,22 +404,22 @@
         functools.partial(build_kernel, rows),
         grid=(rows // ROWS_STEP,),
         out_shape=(
-            jax.ShapeDtypeStruct((rows, named // 2, B, PAIR), bf16),
+            jax.ShapeDtypeStruct((rows, rows // 2, B, PAIR), bf16),
             jax.ShapeDtypeStruct((slots // 4, TILE, TILE), bf16),
-            jax.ShapeDtypeStruct((slots,), jnp.int32),
+            jax.ShapeDtypeStruct((slots + 1,), jnp.int32),
         ),
         in_specs=[smem, smem, pl.BlockSpec((K, ROWS_STEP, B * B), lambda step: (0, step, 0))],
         out_specs=(
-            pl.BlockSpec((ROWS_STEP, named // 2, B, PAIR), lambda step: (step, 0, 0, 0)),
+            pl.BlockSpec((ROWS_STEP, rows // 2, B, PAIR), lambda step: (step, 0, 0, 0)),
             pl.BlockSpec((slots // 4, TILE, TILE), lambda step: (0, 0, 0)),
             smem,
         ),
         scratch_shapes=[
-            pltpu.VMEM((TILE, 2 * TILE), bf16),
+            pltpu.VMEM((TILE, TILE), bf16),
             pltpu.VMEM((TILE, TILE), bf16),
             pltpu.VMEM((3, ROWS_STEP, PAIR), bf16),
             pltpu.VMEM((K, 2, 2, ROWS_STEP, B * B // TILE, PAIR), bf16),
-            pltpu.VMEM((slots, B, PAIR), bf16),
+            pltpu.VMEM((slots + 1, B, PAIR), bf16),
         ],
         compiler_params=pltpu.CompilerParams(vmem_limit_bytes=56 * 1024 * 1024),
     )(by_slot, counts, hblocks.transpose(1, 0, 2))

time: 66.1 us -> 63.7 us (0.964)
  Pallas kernels: 65.3 us -> 62.8 us
    pallas_call x1, Pallas kernels: 17.3 us -> 14.9 us  [on_device(): pl.pallas_call(functools.partial(build_kernel, rows), grid=(rows // ROWS_...]
where the time goes in v6:
time: 63.7 us; the launch traced here: 63.5 us
  Pallas kernels  62.8 us (99%)
  between operations  0.65 us (1%)
    pallas_call x1, Pallas kernels, on_device(): pl.pallas_call(functools.partial(filter_kernel, n_row, n_col), out_shape=...  45.8 us
    pallas_call x1, Pallas kernels, on_device(): pl.pallas_call(functools.partial(build_kernel, rows), grid=(rows // ROWS_...  14.9 us
    pallas_call x1, Pallas kernels, on_device(): pl.pallas_call(functools.partial(output_kernel, cols), out_shape=(jax.Sha...  2.11 us

profile of v6, /device:TPU:0, one launch (start us, length us, event | category | flops | bytes accessed | tf_op | source)
XLA Modules:
  0.0 63.5 jit_solution(5082052254857569702)
XLA Ops:
  0.6 14.9 %shard_map.76 = (bf16[32,16,64,128]{3,2,1,0:T(8,128)(2,1)}, bf16[4,256,256]{2,1,0:T(8,128)(2,1)}, s32[17]{0:T(128)}) custom-call(s32[12,32]{1,0:T(8,128)} %bitcast.5, s32[32]{0:T(128)} %counts.1, bf16[12,32,4096]{2,1,0:T(8,128)(2,1)} %bitcast.4), custom_call_target="tpu_custom_call" | custom-call | tf_op jit(solution)/shard_map/pallas_call | solution.py:403
  15.5 45.8 %shard_map.77 = (bf16[64,2048]{1,0:T(8,128)(2,1)}, bf16[8,16,256]{2,1,0:T(8,128)(2,1)}) custom-call(s32[16]{0:T(128)} %send_rows.1, s32[12,32]{1,0:T(8,128)} %bitcast.6, s32[17]{0:T(128)} %get-tuple-element.11.holder, bf16[64,2048]{1,0:T(8,128)(2,1)} %x_in.1, bf16[4,256,256]{2,1,0:T(8,128)(2,1)} %get-tuple-element.12.diagonal, ...), custom_call_target="tpu_custom_call" | custom-call | tf_op jit(solution)/shard_map/pallas_call | solution.py:427
  61.4 2.1 %shard_map.78 = (bf16[64,2048]{1,0:T(8,128)(2,1)}, f32[64,256]{1,0:T(8,128)}, f32[64,256]{1,0:T(8,128)}) custom-call(bf16[64,2048]{1,0:T(8,128)(2,1)} %get-tuple-element.14.ordered, bf16[8,16,256]{2,1,0:T(8,128)(2,1)} %get-tuple-element.15.sums), custom_call_target="tpu_custom_call" | custom-call | tf_op jit(solution)/shard_map/pallas_call | solution.py:462

commit v7 on v6

--- a/solution.py
+++ b/solution.py
@@ -209,32 +209,41 @@
 
     pl.semaphore_wait(barrier, n_row + n_col - 2)
 
-    def row_copy(phase, slot_here, slot_there, peer):
+    def row_copy(phase, kind, slot_here, slot_there, peer):
         return pltpu.make_async_remote_copy(
-            src_ref=out_buf.at[phase, slot_here],
-            dst_ref=in_buf.at[phase, slot_there],
-            send_sem=send_sem.at[phase, slot_here],
-            recv_sem=recv_sem.at[phase, slot_there],
+            src_ref=out_buf.at[phase, kind, slot_here],
+            dst_ref=in_buf.at[phase, kind, slot_there],
+            send_sem=send_sem.at[phase, kind, slot_here],
+            recv_sem=recv_sem.at[phase, kind, slot_there],
             device_id={"row": peer},
             device_id_type=MESH,
         )
 
+    def send_all(phase, kind):
+        for step in range(1, n_row):
+            peer = lax.rem(me + step, n_row)
+            row_copy(phase, kind, peer, me, peer).start()
+        in_buf[phase, kind, me] = out_buf[phase, kind, me]
+
+    def wait_all(phase, kind):
+        for step in range(1, n_row):
+            peer = lax.rem(me + step, n_row)
+            row_copy(phase, kind, peer, peer, peer).wait_recv()
+
     def pick(first, second):
         return jnp.where(low, blocks[first].astype(f32), blocks[second].astype(f32)).astype(bf16)
 
     def apply_operator(phase, source, finish, beside=None):
+        for peer in range(n_row):
+            out_buf[phase, 0, peer] = pick(send_rows[2 * peer], send_rows[2 * peer + 1])
+        send_all(phase, 0)
         for pack in range(slots // 4):
             at = 4 * pack
             near = jnp.concatenate([pick(holder[at], holder[at + 1]), pick(holder[at + 2], holder[at + 3])], 1)
             product = dot(near, diagonal[pack], NN).astype(bf16)
             for inner in range(2):
-                peer = 2 * pack + inner
-                out_buf[phase, peer, :, pl.ds(0, PAIR)] = pick(send_rows[2 * peer], send_rows[2 * peer + 1])
-                out_buf[phase, peer, :, pl.ds(PAIR, PAIR)] = product[:, inner * PAIR : (inner + 1) * PAIR]
-        for step in range(1, n_row):
-            peer = lax.rem(me + step, n_row)
-            row_copy(phase, peer, me, peer).start()
-        in_buf[phase, me] = out_buf[phase, me]
+                out_buf[phase, 1, 2 * pack + inner] = product[:, inner * PAIR : (inner + 1) * PAIR]
+        send_all(phase, 1)
 
         def local_body(tile, carry):
             down = jnp.concatenate([dense[:, 2 * tile + side].reshape(length, PAIR) for side in range(2)], 1)
@@ -249,23 +258,22 @@
                 dense_copy(tile).wait()
 
         lax.fori_loop(0, tiles, local_body, 0)
-        for step in range(1, n_row):
-            peer = lax.rem(me + step, n_row)
-            row_copy(phase, peer, peer, peer).wait_recv()
-        if beside is not None:
-            beside()
-
+        wait_all(phase, 0)
         for pack in range(slots // 4):
-            far = jnp.concatenate([in_buf[phase, 2 * pack + inner, :, pl.ds(0, PAIR)] for inner in range(2)], 1)
+            far = jnp.concatenate([in_buf[phase, 0, 2 * pack + inner] for inner in range(2)], 1)
             product = dot(far, diagonal[pack], NT)
             for inner in range(2):
                 peer = 2 * pack + inner
                 first, second = both(product[:, inner * PAIR : (inner + 1) * PAIR])
                 upspread[2 * peer] = first
                 upspread[2 * peer + 1] = second
-                first, second = both(in_buf[phase, peer, :, pl.ds(PAIR, PAIR)].astype(f32))
-                spread[2 * peer] = first
-                spread[2 * peer + 1] = second
+        wait_all(phase, 1)
+        for peer in range(n_row):
+            first, second = both(in_buf[phase, 1, peer].astype(f32))
+            spread[2 * peer] = first
+            spread[2 * peer + 1] = second
+        if beside is not None:
+            beside()
 
         def finish_body(pair, carry):
             here = columns(pair, PAIR)
@@ -374,7 +382,8 @@
         sum_copy(peer, peer).wait_recv()
     for peer in peers:
         for phase in range(3):
-            row_copy(phase, peer, me, peer).wait_send()
+            row_copy(phase, 0, peer, me, peer).wait_send()
+            row_copy(phase, 1, peer, me, peer).wait_send()
         piece_copy(peer, me, peer).wait_send()
         sum_copy(me, peer).wait_send()
     for at, peer in enumerate(across):
@@ -442,14 +451,14 @@
             pltpu.VMEM((rows, cols, PAIR), bf16),
             pltpu.VMEM((slots, cols, PAIR), f32),
             pltpu.VMEM((slots + 1, cols, PAIR), f32),
-            pltpu.VMEM((3, n_row, cols, 2 * PAIR), bf16),
-            pltpu.VMEM((3, n_row, cols, 2 * PAIR), bf16),
+            pltpu.VMEM((3, 2, n_row, cols, PAIR), bf16),
+            pltpu.VMEM((3, 2, n_row, cols, PAIR), bf16),
             pltpu.VMEM((n_col, cols, length), bf16),
             pltpu.VMEM((n_row, piece, total_cols), sum_type),
             pltpu.VMEM((n_row, piece, total_cols), sum_type),
             pltpu.VMEM((piece, total_cols), sum_type),
             dma((tiles,)),
-            dma((3, n_row)), dma((3, n_row)),
+            dma((3, 2, n_row)), dma((3, 2, n_row)),
             dma((n_col,)), dma((n_col,)),
             dma((n_row,)), dma((n_row,)),
             dma((n_row,)), dma((n_row,)),

time: 63.7 us -> 63.1 us (level)
  no operation moved by 1% of the time
where the time goes in v7:
time: 63.1 us; the launch traced here: 62.9 us
  Pallas kernels  62.2 us (99%)
  between operations  0.65 us (1%)
    pallas_call x1, Pallas kernels, on_device(): pl.pallas_call(functools.partial(filter_kernel, n_row, n_col), out_shape=...  45.2 us
    pallas_call x1, Pallas kernels, on_device(): pl.pallas_call(functools.partial(build_kernel, rows), grid=(rows // ROWS_...  14.9 us
    pallas_call x1, Pallas kernels, on_device(): pl.pallas_call(functools.partial(output_kernel, cols), out_shape=(jax.Sha...  2.11 us

profile of v7, /device:TPU:0, one launch (start us, length us, event | category | flops | bytes accessed | tf_op | source)
XLA Modules:
  0.0 62.9 jit_solution(2205190887894011985)
XLA Ops:
  0.6 14.9 %shard_map.76 = (bf16[32,16,64,128]{3,2,1,0:T(8,128)(2,1)}, bf16[4,256,256]{2,1,0:T(8,128)(2,1)}, s32[17]{0:T(128)}) custom-call(s32[12,32]{1,0:T(8,128)} %bitcast.5, s32[32]{0:T(128)} %counts.1, bf16[12,32,4096]{2,1,0:T(8,128)(2,1)} %bitcast.4), custom_call_target="tpu_custom_call" | custom-call | tf_op jit(solution)/shard_map/pallas_call | solution.py:412
  15.5 45.2 %shard_map.77 = (bf16[64,2048]{1,0:T(8,128)(2,1)}, bf16[8,16,256]{2,1,0:T(8,128)(2,1)}) custom-call(s32[16]{0:T(128)} %send_rows.1, s32[12,32]{1,0:T(8,128)} %bitcast.6, s32[17]{0:T(128)} %get-tuple-element.11.holder, bf16[64,2048]{1,0:T(8,128)(2,1)} %x_in.1, bf16[4,256,256]{2,1,0:T(8,128)(2,1)} %get-tuple-element.12.diagonal, ...), custom_call_target="tpu_custom_call" | custom-call | tf_op jit(solution)/shard_map/pallas_call | solution.py:436
  60.8 2.1 %shard_map.78 = (bf16[64,2048]{1,0:T(8,128)(2,1)}, f32[64,256]{1,0:T(8,128)}, f32[64,256]{1,0:T(8,128)}) custom-call(bf16[64,2048]{1,0:T(8,128)(2,1)} %get-tuple-element.14.ordered, bf16[8,16,256]{2,1,0:T(8,128)(2,1)} %get-tuple-element.15.sums), custom_call_target="tpu_custom_call" | custom-call | tf_op jit(solution)/shard_map/pallas_call | solution.py:471

commit v8 on v7

--- a/solution.py
+++ b/solution.py
@@ -11,7 +11,7 @@
 K = 12
 PAIR = 2 * B
 TILE = 256
-UNROLL = 8
+UNROLL = 16
 ROWS_STEP = 16
 HALF = B // 2
 

time: 63.1 us -> 63.8 us (1.011)
  Pallas kernels: 62.2 us -> 63 us
    pallas_call x1, Pallas kernels: 14.9 us -> 15.6 us  [on_device(): pl.pallas_call(functools.partial(build_kernel, rows), grid=(rows // ROWS_...]
where the time goes in v8:
time: 63.8 us; the launch traced here: 63.6 us
  Pallas kernels  63 us (99%)
  between operations  0.65 us (1%)
    pallas_call x1, Pallas kernels, on_device(): pl.pallas_call(functools.partial(filter_kernel, n_row, n_col), out_shape=...  45.3 us
    pallas_call x1, Pallas kernels, on_device(): pl.pallas_call(functools.partial(build_kernel, rows), grid=(rows // ROWS_...  15.6 us
    pallas_call x1, Pallas kernels, on_device(): pl.pallas_call(functools.partial(output_kernel, cols), out_shape=(jax.Sha...  2.11 us

profile of v8, /device:TPU:0, one launch (start us, length us, event | category | flops | bytes accessed | tf_op | source)
XLA Modules:
  0.0 63.6 jit_solution(8900391468790673613)
XLA Ops:
  0.6 15.6 %shard_map.76 = (bf16[32,16,64,128]{3,2,1,0:T(8,128)(2,1)}, bf16[4,256,256]{2,1,0:T(8,128)(2,1)}, s32[17]{0:T(128)}) custom-call(s32[12,32]{1,0:T(8,128)} %bitcast.5, s32[32]{0:T(128)} %counts.1, bf16[12,32,4096]{2,1,0:T(8,128)(2,1)} %bitcast.4), custom_call_target="tpu_custom_call" | custom-call | tf_op jit(solution)/shard_map/pallas_call | solution.py:412
  16.2 45.3 %shard_map.77 = (bf16[64,2048]{1,0:T(8,128)(2,1)}, bf16[8,16,256]{2,1,0:T(8,128)(2,1)}) custom-call(s32[16]{0:T(128)} %send_rows.1, s32[12,32]{1,0:T(8,128)} %bitcast.6, s32[17]{0:T(128)} %get-tuple-element.11.holder, bf16[64,2048]{1,0:T(8,128)(2,1)} %x_in.1, bf16[4,256,256]{2,1,0:T(8,128)(2,1)} %get-tuple-element.12.diagonal, ...), custom_call_target="tpu_custom_call" | custom-call | tf_op jit(solution)/shard_map/pallas_call | solution.py:436
  61.5 2.1 %shard_map.78 = (bf16[64,2048]{1,0:T(8,128)(2,1)}, f32[64,256]{1,0:T(8,128)}, f32[64,256]{1,0:T(8,128)}) custom-call(bf16[64,2048]{1,0:T(8,128)(2,1)} %get-tuple-element.14.ordered, bf16[8,16,256]{2,1,0:T(8,128)(2,1)} %get-tuple-element.15.sums), custom_call_target="tpu_custom_call" | custom-call | tf_op jit(solution)/shard_map/pallas_call | solution.py:471
